TPU v7x, 256 devices: a whole 4x4x8 slice. The times are simulated.
256 devices in a mesh: seq: 64 (over y, z, core), tp: 4 (over x).
Axes of the slice: x: 4, y: 4, z: 8, core: 2. Of those that a mesh axis runs over, the one named last changes fastest.
Arguments:
- query_in: bfloat16 [16384, 2048], P('seq', 'tp'), may hold values from -6 to 6
- key_in: bfloat16 [16384, 2048], P('seq', 'tp'), may hold values from -6 to 6
- value_in: bfloat16 [16384, 2048], P('seq', 'tp'), may hold values from -6 to 6
- short_filter: float32 [3, 3, 2048], P(None, None, 'tp'), may hold values from -3 to 3
- skip_gain: float32 [2048], P('tp'), may hold values from 0.5 to 1.5
- filter_taps: float32 [16384, 2048], P('seq', 'tp'), may hold values from -1.2 to 1.2
- out_weight: bfloat16 [2048, 4096], P('tp'), may hold values from -0.125 to 0.125
- out_grad: bfloat16 [16384, 4096], P(('seq', 'tp')), may hold values from -6 to 6
Outputs:
- mixed_out: bfloat16 [16384, 4096], P(('seq', 'tp'))
- grad_query: bfloat16 [16384, 2048], P('seq', 'tp')
- grad_key: bfloat16 [16384, 2048], P('seq', 'tp')
- grad_value: bfloat16 [16384, 2048], P('seq', 'tp')
- filter_grad: float32 [16384, 2048], P('seq', 'tp')
All inputs are finite; a program needn't handle non-finite values.
Results may differ from a plain program's by a relative error of at most 0.015.
Values may be sent and summed in bfloat16 or wider, within the bound.
A program may use at most 128 MiB of HBM per device.

v0:
```python
import math

import jax
import jax.numpy as jnp
from jax import lax
from jax.sharding import PartitionSpec as P

HIGHEST = lax.Precision.HIGHEST


def passed_along(value, axis, steps):
    count = lax.axis_size(axis)
    first, last = (max(0, -steps), min(count, count - steps))
    return lax.ppermute(value, axis, [(source, source + steps) for source in range(first, last)])


def as_sent(x):
    return jax.tree.map(lambda a: a.astype(jnp.bfloat16) if a.dtype == jnp.float32 else a, x)


def split_length(length_all):
    divisor = math.isqrt(length_all)
    while length_all % divisor or divisor % 2:
        divisor -= 1
    return (divisor, length_all // divisor)


def tables(outer_len, inner_len):
    length_all = outer_len * inner_len
    outer_idx = jnp.arange(outer_len, dtype=jnp.int32)
    half_idx = jnp.arange(outer_len // 2, dtype=jnp.int32)
    inner_idx = jnp.arange(inner_len, dtype=jnp.int32)
    outer_angle = (
        -2.0
        * math.pi
        / outer_len
        * (outer_idx[:, None] * half_idx[None, :] % outer_len).astype(jnp.float32)
    )
    twist_angle = (
        -2.0
        * math.pi
        / length_all
        * (outer_idx[:, None] * inner_idx[None, :] % length_all).astype(jnp.float32)
    )
    inner_angle = (
        -2.0
        * math.pi
        / inner_len
        * (inner_idx[:, None] * inner_idx[None, :] % inner_len).astype(jnp.float32)
    )
    return (
        jnp.cos(outer_angle),
        jnp.sin(outer_angle),
        jnp.cos(twist_angle),
        jnp.sin(twist_angle),
        jnp.cos(inner_angle),
        jnp.sin(inner_angle),
    )


def spectrum(signal, table_set):
    outer_cos, outer_sin, twist_cos, twist_sin, inner_cos, inner_sin = table_set
    channels = signal.shape[0]
    folded = signal.reshape(channels, outer_cos.shape[1], inner_cos.shape[0])
    first_re = jnp.einsum("kt,ctn->ckn", outer_cos, folded, precision=HIGHEST)
    first_im = jnp.einsum("kt,ctn->ckn", outer_sin, folded, precision=HIGHEST)
    turned_re = first_re * twist_cos - first_im * twist_sin
    turned_im = first_re * twist_sin + first_im * twist_cos
    spec_re = jnp.einsum("ckn,nm->ckm", turned_re, inner_cos, precision=HIGHEST) - jnp.einsum(
        "ckn,nm->ckm", turned_im, inner_sin, precision=HIGHEST
    )
    spec_im = jnp.einsum("ckn,nm->ckm", turned_re, inner_sin, precision=HIGHEST) + jnp.einsum(
        "ckn,nm->ckm", turned_im, inner_cos, precision=HIGHEST
    )
    return (spec_re, spec_im)


def synthesis(spectra_in, table_set):
    outer_cos, outer_sin, twist_cos, twist_sin, inner_cos, inner_sin = table_set
    spec_re, spec_im = spectra_in
    channels = spec_re.shape[0]
    length_all = outer_cos.shape[0] * inner_cos.shape[0]
    mid_re = jnp.einsum("ckm,mn->ckn", spec_re, inner_cos, precision=HIGHEST) + jnp.einsum(
        "ckm,mn->ckn", spec_im, inner_sin, precision=HIGHEST
    )
    mid_im = jnp.einsum("ckm,mn->ckn", spec_im, inner_cos, precision=HIGHEST) - jnp.einsum(
        "ckm,mn->ckn", spec_re, inner_sin, precision=HIGHEST
    )
    turned_re = mid_re * twist_cos + mid_im * twist_sin
    turned_im = mid_im * twist_cos - mid_re * twist_sin
    result = jnp.einsum("kt,ckn->ctn", outer_cos, turned_re, precision=HIGHEST) + jnp.einsum(
        "kt,ckn->ctn", outer_sin, turned_im, precision=HIGHEST
    )
    return result.reshape(channels, length_all // 2) * (1.0 / length_all)


def complex_times(left, right):
    return (left[0] * right[0] - left[1] * right[1], left[0] * right[1] + left[1] * right[0])


def conj_times(left, right):
    return (left[0] * right[0] + left[1] * right[1], left[0] * right[1] - left[1] * right[0])


def body(query_in, key_in, value_in, short_filter, skip_gain, filter_taps, out_weight, out_grad):
    tok_rows = query_in.shape[0]
    streams = jnp.stack([query_in, key_in, value_in])
    prior_rows = passed_along(streams[:, tok_rows - 2 :, :], "seq", 1)
    extended = jnp.concatenate([prior_rows, streams], axis=1).astype(jnp.float32)
    shortened = (
        short_filter[:, 0:1, :] * extended[:, 2:, :]
        + short_filter[:, 1:2, :] * extended[:, 1:-1, :]
        + short_filter[:, 2:3, :] * extended[:, :-2, :]
    ).astype(jnp.bfloat16)
    q_short = shortened[0].astype(jnp.float32)
    k_short = shortened[1].astype(jnp.float32)
    v_short = shortened[2].astype(jnp.float32)
    signal = k_short * v_short
    seq_len = tok_rows * lax.axis_size("seq")
    outer_len, inner_len = split_length(2 * seq_len)
    table_set = tables(outer_len, inner_len)
    sig_chan, ker_chan = (
        lax.all_to_all(signal.T, "seq", split_axis=0, concat_axis=1, tiled=True),
        lax.all_to_all(filter_taps.T, "seq", split_axis=0, concat_axis=1, tiled=True),
    )
    sig_spec = spectrum(sig_chan, table_set)
    ker_spec = spectrum(ker_chan, table_set)
    conv_chan = synthesis(complex_times(ker_spec, sig_spec), table_set)
    conv_tok = lax.all_to_all(conv_chan, "seq", split_axis=1, concat_axis=0, tiled=True).T
    response = skip_gain * signal + conv_tok
    gate_out = (q_short * response).astype(jnp.bfloat16)
    mixed_out = lax.psum_scatter(
        jnp.dot(gate_out, out_weight, preferred_element_type=jnp.float32).astype(jnp.bfloat16),
        "tp",
        scatter_dimension=0,
        tiled=True,
    )
    grad_gate = lax.dot_general(
        lax.all_gather(out_grad, "tp", axis=0, tiled=True),
        out_weight,
        (((1,), (1,)), ((), ())),
        preferred_element_type=jnp.float32,
    )
    grad_q_short = grad_gate * response
    grad_resp = grad_gate * q_short
    sig_again, ker_again, grad_chan = (
        lax.all_to_all(
            signal.T.astype(jnp.bfloat16), "seq", split_axis=0, concat_axis=1, tiled=True
        ).astype(jnp.float32),
        lax.all_to_all(
            filter_taps.T.astype(jnp.bfloat16), "seq", split_axis=0, concat_axis=1, tiled=True
        ).astype(jnp.float32),
        lax.all_to_all(
            grad_resp.T.astype(jnp.bfloat16), "seq", split_axis=0, concat_axis=1, tiled=True
        ).astype(jnp.float32),
    )
    sig_back = spectrum(sig_again, table_set)
    ker_back = spectrum(ker_again, table_set)
    grad_spec = spectrum(grad_chan, table_set)
    grad_conv = synthesis(conj_times(ker_back, grad_spec), table_set)
    grad_kernel = synthesis(conj_times(sig_back, grad_spec), table_set) * (1.0 / math.sqrt(seq_len))
    back_conv, back_kernel = (
        lax.all_to_all(as_sent(grad_conv), "seq", split_axis=1, concat_axis=0, tiled=True).astype(
            grad_conv.dtype
        ),
        lax.all_to_all(as_sent(grad_kernel), "seq", split_axis=1, concat_axis=0, tiled=True).astype(
            grad_kernel.dtype
        ),
    )
    grad_signal = skip_gain * grad_resp + back_conv.T
    filter_grad = back_kernel.T
    grad_stack = jnp.stack([grad_q_short, grad_signal * v_short, grad_signal * k_short])
    next_rows = passed_along(grad_stack[:, :2, :], "seq", -1)
    grad_ext = jnp.concatenate([grad_stack, next_rows], axis=1)
    stream_grads = (
        short_filter[:, 0:1, :] * grad_ext[:, :-2, :]
        + short_filter[:, 1:2, :] * grad_ext[:, 1:-1, :]
        + short_filter[:, 2:3, :] * grad_ext[:, 2:, :]
    ).astype(jnp.bfloat16)
    return (mixed_out, stream_grads[0], stream_grads[1], stream_grads[2], filter_grad)


def solution(mesh):
    in_specs = (
        P("seq", "tp"),
        P("seq", "tp"),
        P("seq", "tp"),
        P(None, None, "tp"),
        P("tp"),
        P("seq", "tp"),
        P("tp", None),
        P(("seq", "tp"), None),
    )
    out_specs = (
        P(("seq", "tp"), None),
        P("seq", "tp"),
        P("seq", "tp"),
        P("seq", "tp"),
        P("seq", "tp"),
    )
    return jax.shard_map(body, mesh=mesh, in_specs=in_specs, out_specs=out_specs, check_vma=False)
```

profile of v0, /device:TPU:1, one launch (start us, length us, event | category | flops | bytes accessed | tf_op | source)
XLA Modules:
  0.0 271.0 jit_solution(7081215035787369930)
XLA Ops:
  8.0 4.9 %collective-permute-start = (bf16[3,2,512]{2,1,0:T(2,128)(2,1)S(1)}, bf16[3,2,512]{2,1,0:T(2,128)(2,1)S(1)}, u32[]{:S(2)}, u32[]{:S(2)}) collective-permute-start(bf16[3,2,512]{2,1,0:T(2,128)(2,1)S(1)} %pad_maximum_fusion.2), channel_id=1, source_target_pairs={{0,4},{4,8},{8,12},{12,16},{16,20},{20,24},{24,28},{28,32},{32,36}... | collective-permute-start | bytes 18440 | tf_op jit(solution)/shard_map/ppermute | solution.py:14
  14.1 10.9 %all-to-all-start.3 = ((bf16[64,8,256]{2,1,0:T(8,128)(2,1)}), bf16[64,8,256]{2,1,0:T(8,128)(2,1)S(1)}, u32[]{:S(2)}, u32[]{:S(2)}) async-start(bf16[64,8,256]{2,1,0:T(8,128)(2,1)} %fusion.78), calls=%async_computation.4 | async-start | bytes 524288 | tf_op jit(solution)/shard_map/all_to_all | solution.py:150
  26.6 10.4 %all-to-all-done.3 = bf16[64,8,256]{2,1,0:T(8,128)(2,1)S(1)} async-done(((bf16[64,8,256]{2,1,0:T(8,128)(2,1)}), bf16[64,8,256]{2,1,0:T(8,128)(2,1)S(1)}, u32[]{:S(2)}, u32[]{:S(2)}) %all-to-all-start.3) | async-done | bytes 262176 | tf_op jit(solution)/shard_map/all_to_all | solution.py:150
  36.9 6.4 %all-to-all-start = ((f32[64,8,256]{2,1,0:T(8,128)}), f32[64,8,256]{2,1,0:T(8,128)}, u32[]{:S(2)}, u32[]{:S(2)}) async-start(f32[64,8,256]{2,1,0:T(8,128)} %bitcast.295), calls=%async_computation | async-start | bytes 1048576 | tf_op jit(solution)/shard_map/all_to_all | solution.py:124
  49.8 3.0 %convolution_add_fusion.4 = f32[8,128,256]{2,1,0:T(8,128)} fusion(f32[8,128,256]{2,1,0:T(8,128)S(1)} %fusion.16, f32[128,8,256]{2,0,1:T(8,128)S(1)} %fusion.84, f32[128,8,256]{2,0,1:T(8,128)S(1)} %fusion.86, f32[128,256]{1,0:T(8,128)S(1)} %get-tuple-element.37, f32[128,256]{1,0:T(8,128)S(1)} %get-tuple-element.38), kind=kOutput, calls=%fused_computation.27 | convolution fusion | flops 807272448 | bytes 4456448 | tf_op jit(solution)/shard_map/ckn,nm->ckm/dot_general | solution.py:72
  52.8 3.0 %convolution_subtract_fusion.4 = f32[8,128,256]{2,1,0:T(8,128)} fusion(f32[8,128,256]{2,1,0:T(8,128)S(1)} %fusion.18, f32[128,8,256]{2,0,1:T(8,128)S(1)} %fusion.84, f32[128,8,256]{2,0,1:T(8,128)S(1)} %fusion.86, f32[128,256]{1,0:T(8,128)S(1)} %get-tuple-element.37, f32[128,256]{1,0:T(8,128)S(1)} %get-tuple-element.38), kind=kOutput, calls=%fused_computation.29 | convolution fusion | flops 807272448 | bytes 4456448 | tf_op jit(solution)/shard_map/ckn,nm->ckm/dot_general | solution.py:69
  55.8 4.6 %all-to-all-done = f32[64,8,256]{2,1,0:T(8,128)} async-done(((f32[64,8,256]{2,1,0:T(8,128)}), f32[64,8,256]{2,1,0:T(8,128)}, u32[]{:S(2)}, u32[]{:S(2)}) %all-to-all-start) | async-done | bytes 524320 | tf_op jit(solution)/shard_map/all_to_all | solution.py:124
  60.4 2.2 fusion.52
  62.6 2.4 fusion.54
  65.0 3.0 %fusion.24 = f32[8,128,256]{2,1,0:T(8,128)} fusion(f32[128,8,256]{2,0,1:T(8,128)S(1)} %fusion.52, f32[128,8,256]{2,0,1:T(8,128)S(1)} %fusion.54, f32[128,256]{1,0:T(8,128)S(1)} %get-tuple-element.37, f32[128,256]{1,0:T(8,128)S(1)} %get-tuple-element.38), kind=kOutput, calls=%fused_computation.57 | convolution fusion | flops 807010304 | bytes 3407872 | tf_op jit(solution)/shard_map/ckn,nm->ckm/dot_general | solution.py:69
  68.0 4.1 %fusion.417 = f32[256,512]{1,0:T(8,128)S(1)} fusion(bf16[256,4096]{1,0:T(8,128)(2,1)} %all-gather.2.cloned.1.call-done, bf16[512,4096]{1,0:T(8,128)(2,1)} %param.14), kind=kOutput, calls=%fused_computation.449 | convolution fusion | flops 1073741824 | bytes 6815744 | tf_op jit(solution)/shard_map/dot_general | solution.py:138
  75.1 6.3 %all-to-all-start.4 = ((bf16[64,8,256]{2,1,0:T(8,128)(2,1)}), bf16[64,8,256]{2,1,0:T(8,128)(2,1)S(1)}, u32[]{:S(2)}, u32[]{:S(2)}) async-start(bf16[64,8,256]{2,1,0:T(8,128)(2,1)} %bitcast.31), calls=%async_computation.5 | async-start | bytes 524288 | tf_op jit(solution)/shard_map/all_to_all | solution.py:153
  81.4 3.0 %fusion.22 = f32[8,128,256]{2,1,0:T(8,128)} fusion(f32[128,8,256]{2,0,1:T(8,128)S(1)} %fusion.52, f32[128,8,256]{2,0,1:T(8,128)S(1)} %fusion.54, f32[128,256]{1,0:T(8,128)S(1)} %get-tuple-element.37, f32[128,256]{1,0:T(8,128)S(1)} %get-tuple-element.38), kind=kOutput, calls=%fused_computation.55 | convolution fusion | flops 807010304 | bytes 3407872 | tf_op jit(solution)/shard_map/ckn,nm->ckm/dot_general | solution.py:72
  84.4 3.0 %convolution_subtract_fusion.7 = f32[8,128,256]{2,1,0:T(8,128)} fusion(f32[8,128,256]{2,1,0:T(8,128)S(1)} %copy-done.19, f32[128,8,256]{2,0,1:T(8,128)S(1)} %fusion.52, f32[128,8,256]{2,0,1:T(8,128)S(1)} %fusion.54, f32[128,256]{1,0:T(8,128)S(1)} %get-tuple-element.37, f32[128,256]{1,0:T(8,128)S(1)} %get-tuple-element.38), kind=kOutput, calls=%fused_computation.35 | convolution fusion | flops 807272448 | bytes 4456448 | tf_op jit(solution)/shard_map/ckn,nm->ckm/dot_general | solution.py:69
  90.2 3.1 %all-to-all-done.4 = bf16[64,8,256]{2,1,0:T(8,128)(2,1)S(1)} async-done(((bf16[64,8,256]{2,1,0:T(8,128)(2,1)}), bf16[64,8,256]{2,1,0:T(8,128)(2,1)S(1)}, u32[]{:S(2)}, u32[]{:S(2)}) %all-to-all-start.4) | async-done | bytes 262176 | tf_op jit(solution)/shard_map/all_to_all | solution.py:153
  93.4 7.7 %all-to-all-start.6 = ((bf16[64,8,256]{2,1,0:T(8,128)(2,1)}), bf16[64,8,256]{2,1,0:T(8,128)(2,1)S(1)}, u32[]{:S(2)}, u32[]{:S(2)}) async-start(bf16[64,8,256]{2,1,0:T(8,128)(2,1)} %bitcast.46), calls=%async_computation.7 | async-start | bytes 524288 | tf_op jit(solution)/shard_map/all_to_all | solution.py:147
  102.6 3.7 %fusion.95 = f32[8,128,256]{2,1,0:T(8,128)} fusion(f32[8,128,256]{1,2,0:T(8,128)S(1)} %convolution_bitcast_fusion.4, f32[8,128,256]{1,2,0:T(8,128)S(1)} %convolution_bitcast_fusion.5, f32[128,256]{0,1:T(8,128)S(1)} %copy.99, f32[128,256]{0,1:T(8,128)S(1)} %copy.98), kind=kOutput, calls=%fused_computation.164 | convolution fusion | flops 807010304 | bytes 3407872 | tf_op jit(solution)/shard_map/ckn,nm->ckm/dot_general | solution.py:72
  106.3 3.8 %fusion.120 = f32[8,128,256]{2,1,0:T(8,128)} fusion(f32[8,128,256]{1,2,0:T(8,128)S(1)} %convolution_bitcast_fusion.4, f32[8,128,256]{1,2,0:T(8,128)S(1)} %convolution_bitcast_fusion.5, f32[128,256]{0,1:T(8,128)S(1)} %copy.99, f32[128,256]{0,1:T(8,128)S(1)} %copy.98), kind=kOutput, calls=%fused_computation.189 | convolution fusion | flops 807010304 | bytes 3407872 | tf_op jit(solution)/shard_map/ckn,nm->ckm/dot_general | solution.py:69
  110.1 2.8 %all-to-all-done.6 = bf16[64,8,256]{2,1,0:T(8,128)(2,1)S(1)} async-done(((bf16[64,8,256]{2,1,0:T(8,128)(2,1)}), bf16[64,8,256]{2,1,0:T(8,128)(2,1)S(1)}, u32[]{:S(2)}, u32[]{:S(2)}) %all-to-all-start.6) | async-done | bytes 262176 | tf_op jit(solution)/shard_map/all_to_all | solution.py:147
  113.7 7.9 %all-to-all-start.1 = ((f32[64,8,256]{2,1,0:T(8,128)}), f32[64,8,256]{2,1,0:T(8,128)}, u32[]{:S(2)}, u32[]{:S(2)}) async-start(f32[64,8,256]{2,1,0:T(8,128)} %bitcast.296), calls=%async_computation.1 | async-start | bytes 1048576 | tf_op jit(solution)/shard_map/all_to_all | solution.py:123
  124.9 2.7 %fusion.112 = f32[8,128,256]{2,1,0:T(8,128)S(1)} fusion(f32[8,128,256]{1,2,0:T(8,128)S(1)} %convolution_bitcast_fusion.2, f32[8,128,256]{1,2,0:T(8,128)S(1)} %convolution_bitcast_fusion.3, f32[128,256]{0,1:T(8,128)S(1)} %copy.99, f32[128,256]{0,1:T(8,128)S(1)} %copy.98), kind=kOutput, calls=%fused_computation.181 | convolution fusion | flops 807010304 | bytes 3407872 | tf_op jit(solution)/shard_map/ckn,nm->ckm/dot_general | solution.py:69
  127.7 3.7 %fusion.90 = f32[8,128,256]{2,1,0:T(8,128)} fusion(f32[8,128,256]{1,2,0:T(8,128)S(1)} %convolution_bitcast_fusion.2, f32[8,128,256]{1,2,0:T(8,128)S(1)} %convolution_bitcast_fusion.3, f32[128,256]{0,1:T(8,128)S(1)} %copy.99, f32[128,256]{0,1:T(8,128)S(1)} %copy.98), kind=kOutput, calls=%fused_computation.159 | convolution fusion | flops 807010304 | bytes 3407872 | tf_op jit(solution)/shard_map/ckn,nm->ckm/dot_general | solution.py:72
  131.5 3.7 %convolution_add_fusion.3 = f32[8,128,256]{2,1,0:T(8,128)} fusion(f32[8,128,256]{2,1,0:T(8,128)S(1)} %copy-done.20, f32[8,128,256]{1,2,0:T(8,128)S(1)} %copy-done.3, f32[8,128,256]{1,2,0:T(8,128)S(1)} %copy-done.5, f32[128,256]{0,1:T(8,128)S(1)} %copy.99, f32[128,256]{0,1:T(8,128)S(1)} %copy.98), kind=kOutput, calls=%fused_computation.26 | convolution fusion | flops 807272448 | bytes 4456448 | tf_op jit(solution)/shard_map/ckn,nm->ckm/dot_general | solution.py:72
  135.2 3.9 %convolution_subtract_fusion.1 = f32[8,128,256]{2,1,0:T(8,128)} fusion(f32[8,128,256]{2,1,0:T(8,128)S(1)} %fusion.112, f32[8,128,256]{1,2,0:T(8,128)S(1)} %convolution_bitcast_fusion.2, f32[8,128,256]{1,2,0:T(8,128)S(1)} %convolution_bitcast_fusion.3, f32[128,256]{0,1:T(8,128)S(1)} %copy.99, f32[128,256]{0,1:T(8,128)S(1)} %copy.98), kind=kOutput, calls=%fused_computation.23 | convolution fusion | flops 807272448 | bytes 4456448 | tf_op jit(solution)/shard_map/ckn,nm->ckm/dot_general | solution.py:69
  139.1 3.8 %convolution_subtract_fusion.3 = f32[8,128,256]{2,1,0:T(8,128)} fusion(f32[8,128,256]{2,1,0:T(8,128)S(1)} %copy-done.18, f32[8,128,256]{1,2,0:T(8,128)S(1)} %copy-done.3, f32[8,128,256]{1,2,0:T(8,128)S(1)} %copy-done.5, f32[128,256]{0,1:T(8,128)S(1)} %copy.99, f32[128,256]{0,1:T(8,128)S(1)} %copy.98), kind=kOutput, calls=%fused_computation.28 | convolution fusion | flops 807272448 | bytes 4456448 | tf_op jit(solution)/shard_map/ckn,nm->ckm/dot_general | solution.py:69
  142.9 2.9 %convolution_bitcast_fusion = f32[8,128,256]{1,2,0:T(8,128)S(1)} fusion(f32[64,8,256]{2,1,0:T(8,128)} %all-to-all-done.1), kind=kOutput, calls=%fused_computation.14 | convolution fusion | flops 201441280 | bytes 1572864 | tf_op jit(solution)/shard_map/kt,ctn->ckn/dot_general | solution.py:66
  145.9 2.9 %convolution_bitcast_fusion.1 = f32[8,128,256]{1,2,0:T(8,128)S(1)} fusion(f32[64,8,256]{2,1,0:T(8,128)} %all-to-all-done.1), kind=kOutput, calls=%fused_computation.15 | convolution fusion | flops 201441280 | bytes 1572864 | tf_op jit(solution)/shard_map/kt,ctn->ckn/dot_general | solution.py:65
  148.8 2.7 %fusion.102 = f32[8,128,256]{2,1,0:T(8,128)S(1)} fusion(f32[8,128,256]{1,2,0:T(8,128)S(1)} %convolution_bitcast_fusion, f32[8,128,256]{1,2,0:T(8,128)S(1)} %convolution_bitcast_fusion.1, f32[128,256]{0,1:T(8,128)S(1)} %copy.99, f32[128,256]{0,1:T(8,128)S(1)} %copy.98), kind=kOutput, calls=%fused_computation.171 | convolution fusion | flops 807010304 | bytes 3407872 | tf_op jit(solution)/shard_map/ckn,nm->ckm/dot_general | solution.py:72
  151.6 3.1 %fusion.129 = f32[8,128,256]{2,1,0:T(8,128)S(1)} fusion(f32[8,128,256]{1,2,0:T(8,128)S(1)} %convolution_bitcast_fusion, f32[8,128,256]{1,2,0:T(8,128)S(1)} %convolution_bitcast_fusion.1, f32[128,256]{0,1:T(8,128)S(1)} %copy.99, f32[128,256]{0,1:T(8,128)S(1)} %copy.98), kind=kOutput, calls=%fused_computation.198 | convolution fusion | flops 807010304 | bytes 3407872 | tf_op jit(solution)/shard_map/ckn,nm->ckm/dot_general | solution.py:69
  154.7 2.7 %convolution_add_fusion.6 = f32[8,128,256]{2,1,0:T(8,128)S(1)} fusion(f32[8,128,256]{2,1,0:T(8,128)S(1)} %fusion.102, f32[8,128,256]{1,2,0:T(8,128)S(1)} %convolution_bitcast_fusion, f32[8,128,256]{1,2,0:T(8,128)S(1)} %convolution_bitcast_fusion.1, f32[128,256]{0,1:T(8,128)S(1)} %copy.99, f32[128,256]{0,1:T(8,128)S(1)} %copy.98), kind=kOutput, calls=%fused_computation.32 | convolution fusion | flops 807272448 | bytes 4456448 | tf_op jit(solution)/shard_map/ckn,nm->ckm/dot_general | solution.py:72
  157.5 2.8 %convolution_subtract_fusion.6 = f32[8,128,256]{2,1,0:T(8,128)S(1)} fusion(f32[8,128,256]{2,1,0:T(8,128)S(1)} %fusion.129, f32[8,128,256]{1,2,0:T(8,128)S(1)} %convolution_bitcast_fusion, f32[8,128,256]{1,2,0:T(8,128)S(1)} %convolution_bitcast_fusion.1, f32[128,256]{0,1:T(8,128)S(1)} %copy.99, f32[128,256]{0,1:T(8,128)S(1)} %copy.98), kind=kOutput, calls=%fused_computation.34 | convolution fusion | flops 807272448 | bytes 4456448 | tf_op jit(solution)/shard_map/ckn,nm->ckm/dot_general | solution.py:69
  160.3 2.2 multiply_subtract_fusion.5
  164.6 2.2 fusion.125
  166.9 2.1 convolution_subtract_fusion.5
  169.0 2.1 convolution_add_fusion.5
  175.2 10.5 %all-to-all-start.2 = ((f32[8,64,256]{2,0,1:T(8,128)}), f32[8,64,256]{2,0,1:T(8,128)}, u32[]{:S(2)}, u32[]{:S(2)}) async-start(f32[8,64,256]{2,0,1:T(8,128)} %copy.110), calls=%async_computation.2 | async-start | bytes 1048576 | tf_op jit(solution)/shard_map/all_to_all | solution.py:129
  186.1 6.9 %multiply_add_fusion = (f32[8,128,256]{2,1,0:T(8,128)}, f32[8,128,256]{2,1,0:T(8,128)S(1)}, f32[8,128,256]{2,1,0:T(8,128)S(1)}, f32[8,128,256]{2,1,0:T(8,128)S(1)}) fusion(f32[8,128,256]{2,1,0:T(8,128)} %convolution_add_fusion.3, f32[8,128,256]{2,1,0:T(8,128)} %convolution_subtract_fusion.1, f32[8,128,256]{2,1,0:T(8,128)} %convolution_subtract_fusion.3, ...), kind=kOutput, calls=%fused_computation.67 | convolution fusion | flops 810418176 | bytes 12845056 | tf_op jit(solution)/shard_map/ckn,nm->ckm/dot_general | solution.py:72
  193.0 2.1 fusion.114
  195.1 3.0 %fusion.116 = f32[8,128,256]{1,2,0:T(8,128)} fusion(f32[8,128,256]{2,1,0:T(8,128)S(1)} %get-tuple-element.22), kind=kOutput, calls=%fused_computation.185 | convolution fusion | flops 806223872 | bytes 2097152 | tf_op jit(solution)/shard_map/ckm,mn->ckn/dot_general | solution.py:83
  200.2 2.7 %all-to-all-done.2 = f32[8,64,256]{2,0,1:T(8,128)} async-done(((f32[8,64,256]{2,0,1:T(8,128)}), f32[8,64,256]{2,0,1:T(8,128)}, u32[]{:S(2)}, u32[]{:S(2)}) %all-to-all-start.2) | async-done | bytes 524320 | tf_op jit(solution)/shard_map/all_to_all | solution.py:129
  205.0 5.1 %convolution_convert_fusion = bf16[256,4096]{1,0:T(8,128)(2,1)} fusion(bf16[512,4096]{1,0:T(8,128)(2,1)} %param.14, bf16[3,256,512]{2,1,0:T(8,128)(2,1)} %copy-done.11, f32[512,256]{0,1:T(8,128)S(1)} %copy.111, f32[512]{0:T(512)S(1)} %copy-done.32), kind=kOutput, calls=%fused_computation | convolution fusion | flops 1075838976 | bytes 7604224 | tf_op jit(solution)/shard_map/dot_general | solution.py:133
  211.3 3.3 %convolution_add_fusion.2 = f32[8,128,256]{1,2,0:T(8,128)S(1)} fusion(f32[8,128,256]{1,2,0:T(8,128)} %fusion.116, f32[8,128,256]{2,1,0:T(8,128)S(1)} %copy-done.10), kind=kOutput, calls=%fused_computation.25 | convolution fusion | flops 806486016 | bytes 3145728 | tf_op jit(solution)/shard_map/ckm,mn->ckn/dot_general | solution.py:83
  218.4 7.9 %all-to-all-start.5 = ((bf16[8,64,256]{2,0,1:T(8,128)(2,1)}), bf16[8,64,256]{2,0,1:T(8,128)(2,1)S(1)}, u32[]{:S(2)}, u32[]{:S(2)}) async-start(bf16[8,64,256]{2,0,1:T(8,128)(2,1)} %copy.125), calls=%async_computation.6 | async-start | bytes 524288 | tf_op jit(solution)/shard_map/all_to_all | solution.py:163
  230.5 2.1 convolution_subtract_fusion
  232.6 2.1 convolution_add_fusion
  238.5 10.3 %all-to-all-start.7 = ((bf16[8,64,256]{2,0,1:T(8,128)(2,1)}), bf16[8,64,256]{2,0,1:T(8,128)(2,1)S(1)}, u32[]{:S(2)}, u32[]{:S(2)}) async-start(bf16[8,64,256]{2,0,1:T(8,128)(2,1)} %copy.139), calls=%async_computation.8 | async-start | bytes 524288 | tf_op jit(solution)/shard_map/all_to_all | solution.py:166
  251.6 2.4 collective-permute-start.1
  253.9 6.9 %all-to-all-done.7 = bf16[8,64,256]{2,0,1:T(8,128)(2,1)S(1)} async-done(((bf16[8,64,256]{2,0,1:T(8,128)(2,1)}), bf16[8,64,256]{2,0,1:T(8,128)(2,1)S(1)}, u32[]{:S(2)}, u32[]{:S(2)}) %all-to-all-start.7) | async-done | bytes 262176 | tf_op jit(solution)/shard_map/all_to_all | solution.py:166
  (123 shorter events, 50.7 us)
Async XLA Ops:
  7.2 5.8 %copy-start.28 = (f32[256,512]{1,0:T(8,128)S(1)}, f32[256,512]{1,0:T(8,128)}, u32[]{:S(2)}) copy-start(f32[256,512]{1,0:T(8,128)} %param.13) | copy-start | bytes 1572868
  7.2 60.9 %all-gather.2.cloned.1.call-start = ((), (), s32[]{:S(2)}) async-start(), calls=%async_computation.10 | async-start | bytes 2621440 | tf_op jit(solution)/shard_map/all_gather | solution.py:139
  8.0 16.9 %copy-start.31 = (f32[3,3,512]{2,1,0:T(4,128)S(1)}, f32[3,3,512]{2,1,0:T(4,128)}, u32[]{:S(2)}) copy-start(f32[3,3,512]{2,1,0:T(4,128)} %param.11) | copy-start | bytes 55300
  8.0 17.7 %collective-permute-start = (bf16[3,2,512]{2,1,0:T(2,128)(2,1)S(1)}, bf16[3,2,512]{2,1,0:T(2,128)(2,1)S(1)}, u32[]{:S(2)}, u32[]{:S(2)}) collective-permute-start(bf16[3,2,512]{2,1,0:T(2,128)(2,1)S(1)} %pad_maximum_fusion.2), channel_id=1, source_target_pairs={{0,4},{4,8},{8,12},{12,16},{16,20},{20,24},{24,28},{28,32},{32,36}... | collective-permute-start | bytes 18440 | tf_op jit(solution)/shard_map/ppermute | solution.py:14
  13.0 12.8 %copy-start.25 = (bf16[256,512]{1,0:T(8,128)(2,1)S(1)}, bf16[256,512]{1,0:T(8,128)(2,1)}, u32[]{:S(2)}) copy-start(bf16[256,512]{1,0:T(8,128)(2,1)} %param.10) | copy-start | bytes 786436
  13.0 12.8 %copy-start.26 = (bf16[256,512]{1,0:T(8,128)(2,1)S(1)}, bf16[256,512]{1,0:T(8,128)(2,1)}, u32[]{:S(2)}) copy-start(bf16[256,512]{1,0:T(8,128)(2,1)} %param.9) | copy-start | bytes 786436
  13.0 12.8 %copy-start.27 = (bf16[256,512]{1,0:T(8,128)(2,1)S(1)}, bf16[256,512]{1,0:T(8,128)(2,1)}, u32[]{:S(2)}) copy-start(bf16[256,512]{1,0:T(8,128)(2,1)} %param.8) | copy-start | bytes 786436
  13.2 11.7 %copy-start.13 = (f32[256,512]{0,1:T(8,128)}, f32[256,512]{0,1:T(8,128)S(1)}, u32[]{:S(2)}) copy-start(f32[256,512]{0,1:T(8,128)S(1)} %copy.94) | copy-start | bytes 1572868
  14.1 22.9 %all-to-all-start.3 = ((bf16[64,8,256]{2,1,0:T(8,128)(2,1)}), bf16[64,8,256]{2,1,0:T(8,128)(2,1)S(1)}, u32[]{:S(2)}, u32[]{:S(2)}) async-start(bf16[64,8,256]{2,1,0:T(8,128)(2,1)} %fusion.78), calls=%async_computation.4 | async-start | bytes 524288 | tf_op jit(solution)/shard_map/all_to_all | solution.py:150
  25.5 58.9 %copy-start.6 = (f32[128,256]{1,0:T(8,128)}, f32[128,256]{1,0:T(8,128)S(1)}, u32[]{:S(2)}) copy-start(f32[128,256]{1,0:T(8,128)S(1)} %get-tuple-element.38) | copy-start | bytes 393220
  25.5 1.0 copy-start.29
  26.5 45.6 %copy-start.11 = (bf16[3,256,512]{2,1,0:T(8,128)(2,1)}, bf16[3,256,512]{2,1,0:T(8,128)(2,1)S(1)}, u32[]{:S(2)}) copy-start(bf16[3,256,512]{2,1,0:T(8,128)(2,1)S(1)} %fusion.4) | copy-start | bytes 2359300
  36.9 6.4 %copy-start.21 = (bf16[64,8,256]{2,1,0:T(8,128)(2,1)}, bf16[64,8,256]{2,1,0:T(8,128)(2,1)S(1)}, u32[]{:S(2)}) copy-start(bf16[64,8,256]{2,1,0:T(8,128)(2,1)S(1)} %all-to-all-done.3) | copy-start | bytes 786436
  36.9 23.5 %all-to-all-start = ((f32[64,8,256]{2,1,0:T(8,128)}), f32[64,8,256]{2,1,0:T(8,128)}, u32[]{:S(2)}, u32[]{:S(2)}) async-start(f32[64,8,256]{2,1,0:T(8,128)} %bitcast.295), calls=%async_computation | async-start | bytes 1048576 | tf_op jit(solution)/shard_map/all_to_all | solution.py:124
  72.2 1.1 copy-start.23
  75.1 18.3 %all-to-all-start.4 = ((bf16[64,8,256]{2,1,0:T(8,128)(2,1)}), bf16[64,8,256]{2,1,0:T(8,128)(2,1)S(1)}, u32[]{:S(2)}, u32[]{:S(2)}) async-start(bf16[64,8,256]{2,1,0:T(8,128)(2,1)} %bitcast.31), calls=%async_computation.5 | async-start | bytes 524288 | tf_op jit(solution)/shard_map/all_to_all | solution.py:153
  81.4 3.1 %copy-start.19 = (f32[8,128,256]{2,1,0:T(8,128)S(1)}, f32[8,128,256]{2,1,0:T(8,128)}, u32[]{:S(2)}) copy-start(f32[8,128,256]{2,1,0:T(8,128)} %fusion.24) | copy-start | bytes 3145732
  84.4 3.0 %copy-start.24 = (f32[512,256]{0,1:T(8,128)S(1)}, f32[512,256]{0,1:T(8,128)}, u32[]{:S(2)}) copy-start(f32[512,256]{0,1:T(8,128)} %get-tuple-element.27) | copy-start | bytes 1572868
  93.4 19.6 %all-to-all-start.6 = ((bf16[64,8,256]{2,1,0:T(8,128)(2,1)}), bf16[64,8,256]{2,1,0:T(8,128)(2,1)S(1)}, u32[]{:S(2)}, u32[]{:S(2)}) async-start(bf16[64,8,256]{2,1,0:T(8,128)(2,1)} %bitcast.46), calls=%async_computation.7 | async-start | bytes 524288 | tf_op jit(solution)/shard_map/all_to_all | solution.py:147
  101.8 4.5 %copy-start.2 = (f32[8,128,256]{1,2,0:T(8,128)}, f32[8,128,256]{1,2,0:T(8,128)S(1)}, u32[]{:S(2)}) copy-start(f32[8,128,256]{1,2,0:T(8,128)S(1)} %convolution_bitcast_fusion.4) | copy-start | bytes 3145732
  102.6 3.8 %copy-start.4 = (f32[8,128,256]{1,2,0:T(8,128)}, f32[8,128,256]{1,2,0:T(8,128)S(1)}, u32[]{:S(2)}) copy-start(f32[8,128,256]{1,2,0:T(8,128)S(1)} %convolution_bitcast_fusion.5) | copy-start | bytes 3145732
  113.0 0.7 copy-start.22
  113.7 29.3 %all-to-all-start.1 = ((f32[64,8,256]{2,1,0:T(8,128)}), f32[64,8,256]{2,1,0:T(8,128)}, u32[]{:S(2)}, u32[]{:S(2)}) async-start(f32[64,8,256]{2,1,0:T(8,128)} %bitcast.296), calls=%async_computation.1 | async-start | bytes 1048576 | tf_op jit(solution)/shard_map/all_to_all | solution.py:123
  124.9 10.2 %copy-start = (f32[8,128,256]{1,2,0:T(8,128)}, f32[8,128,256]{1,2,0:T(8,128)S(1)}, u32[]{:S(2)}) copy-start(f32[8,128,256]{1,2,0:T(8,128)S(1)} %convolution_bitcast_fusion.3) | copy-start | bytes 3145732
  127.7 3.8 %copy-start.3 = (f32[8,128,256]{1,2,0:T(8,128)S(1)}, f32[8,128,256]{1,2,0:T(8,128)}, u32[]{:S(2)}) copy-start(f32[8,128,256]{1,2,0:T(8,128)} %copy-done.2) | copy-start | bytes 3145732
  127.7 3.8 %copy-start.5 = (f32[8,128,256]{1,2,0:T(8,128)S(1)}, f32[8,128,256]{1,2,0:T(8,128)}, u32[]{:S(2)}) copy-start(f32[8,128,256]{1,2,0:T(8,128)} %copy-done.4) | copy-start | bytes 3145732
  127.7 3.8 %copy-start.20 = (f32[8,128,256]{2,1,0:T(8,128)S(1)}, f32[8,128,256]{2,1,0:T(8,128)}, u32[]{:S(2)}) copy-start(f32[8,128,256]{2,1,0:T(8,128)} %fusion.95) | copy-start | bytes 3145732
  135.2 3.9 %copy-start.18 = (f32[8,128,256]{2,1,0:T(8,128)S(1)}, f32[8,128,256]{2,1,0:T(8,128)}, u32[]{:S(2)}) copy-start(f32[8,128,256]{2,1,0:T(8,128)} %fusion.120) | copy-start | bytes 3145732
  157.5 2.8 %copy-start.7 = (f32[128,256]{1,0:T(8,128)S(1)}, f32[128,256]{1,0:T(8,128)}, u32[]{:S(2)}) copy-start(f32[128,256]{1,0:T(8,128)} %copy-done.6) | copy-start | bytes 393220
  157.5 2.8 %copy-start.16 = (f32[8,128,256]{2,1,0:T(8,128)S(1)}, f32[8,128,256]{2,1,0:T(8,128)}, u32[]{:S(2)}) copy-start(f32[8,128,256]{2,1,0:T(8,128)} %convolution_subtract_fusion.7) | copy-start | bytes 3145732
  157.5 2.8 %copy-start.17 = (f32[8,128,256]{2,1,0:T(8,128)S(1)}, f32[8,128,256]{2,1,0:T(8,128)}, u32[]{:S(2)}) copy-start(f32[8,128,256]{2,1,0:T(8,128)} %fusion.22) | copy-start | bytes 3145732
  174.0 12.1 %copy-start.1 = (f32[8,128,256]{1,2,0:T(8,128)S(1)}, f32[8,128,256]{1,2,0:T(8,128)}, u32[]{:S(2)}) copy-start(f32[8,128,256]{1,2,0:T(8,128)} %copy-done) | copy-start | bytes 3145732
  175.2 27.8 %all-to-all-start.2 = ((f32[8,64,256]{2,0,1:T(8,128)}), f32[8,64,256]{2,0,1:T(8,128)}, u32[]{:S(2)}, u32[]{:S(2)}) async-start(f32[8,64,256]{2,0,1:T(8,128)} %copy.110), calls=%async_computation.2 | async-start | bytes 1048576 | tf_op jit(solution)/shard_map/all_to_all | solution.py:129
  185.7 78.3 %reduce-scatter.2.cloned.1.call-start = ((), (), s32[]{:S(2)}) async-start(), calls=%async_computation.9 | async-start | bytes 2621440 | tf_op jit(solution)/shard_map/reduce_scatter | solution.py:132
  193.0 5.1 %copy-start.9 = (f32[8,128,256]{2,1,0:T(8,128)}, f32[8,128,256]{2,1,0:T(8,128)S(1)}, u32[]{:S(2)}) copy-start(f32[8,128,256]{2,1,0:T(8,128)S(1)} %get-tuple-element.21) | copy-start | bytes 3145732
  198.1 6.9 %copy-start.32 = (f32[512]{0:T(512)S(1)}, f32[512]{0:T(512)}, u32[]{:S(2)}) copy-start(f32[512]{0:T(512)} %param.12) | copy-start | bytes 6148
  204.2 0.8 copy-start.14
  210.1 1.2 copy-start.10
  217.6 10.8 %copy-start.8 = (f32[8,128,256]{2,1,0:T(8,128)S(1)}, f32[8,128,256]{2,1,0:T(8,128)}, u32[]{:S(2)}) copy-start(f32[8,128,256]{2,1,0:T(8,128)} %get-tuple-element.15) | copy-start | bytes 3145732
  218.4 20.1 %all-to-all-start.5 = ((bf16[8,64,256]{2,0,1:T(8,128)(2,1)}), bf16[8,64,256]{2,0,1:T(8,128)(2,1)S(1)}, u32[]{:S(2)}, u32[]{:S(2)}) async-start(bf16[8,64,256]{2,0,1:T(8,128)(2,1)} %copy.125), calls=%async_computation.6 | async-start | bytes 524288 | tf_op jit(solution)/shard_map/all_to_all | solution.py:163
  237.7 12.2 %copy-start.12 = (bf16[3,256,512]{2,1,0:T(8,128)(2,1)S(1)}, bf16[3,256,512]{2,1,0:T(8,128)(2,1)}, u32[]{:S(2)}) copy-start(bf16[3,256,512]{2,1,0:T(8,128)(2,1)} %copy-done.11) | copy-start | bytes 2359300
  237.7 12.2 %copy-start.15 = (f32[512,256]{0,1:T(8,128)S(1)}, f32[512,256]{0,1:T(8,128)}, u32[]{:S(2)}) copy-start(f32[512,256]{0,1:T(8,128)} %copy-done.14) | copy-start | bytes 1572868
  238.5 22.3 %all-to-all-start.7 = ((bf16[8,64,256]{2,0,1:T(8,128)(2,1)}), bf16[8,64,256]{2,0,1:T(8,128)(2,1)S(1)}, u32[]{:S(2)}, u32[]{:S(2)}) async-start(bf16[8,64,256]{2,0,1:T(8,128)(2,1)} %copy.139), calls=%async_computation.8 | async-start | bytes 524288 | tf_op jit(solution)/shard_map/all_to_all | solution.py:166
  251.6 10.3 %collective-permute-start.1 = (f32[3,2,512]{2,1,0:T(2,128)S(1)}, f32[3,2,512]{2,1,0:T(2,128)S(1)}, u32[]{:S(2)}, u32[]{:S(2)}) collective-permute-start(f32[3,2,512]{2,1,0:T(2,128)S(1)} %slice.73), channel_id=1, source_target_pairs={{4,0},{8,4},{12,8},{16,12},{20,16},{24,20},{28,24},{32,28},{36,32}... | collective-permute-start | bytes 36872 | tf_op jit(solution)/shard_map/ppermute | solution.py:14
  261.9 0.7 copy-start.30
Sparse Core Ops, SparseCore 0:
  13.1 34.9 all-gather.1
  210.2 30.4 reduce-scatter.1
where the time goes:
time: 276 us; the launch traced here: 271 us
  matrix products  128 us (46%)
  starting transfers between devices  75.6 us (27%)
  waiting for transfers between devices  30.7 us (11%)
  local copies, waits for them, and re-layouts  15.3 us (6%)
  between operations  15 us (5%)
  other arithmetic  6.35 us (2%)
    dot_general x5, matrix products, spectrum(): jnp.einsum('ckn,nm->ckm', turned_im, inner_cos, precision=HIGHEST)  18.5 us
    dot_general x5, matrix products, spectrum(): jnp.einsum('ckn,nm->ckm', turned_im, inner_sin, precision=HIGHEST)  16.5 us
    dot_general x5, matrix products, spectrum(): jnp.einsum('ckn,nm->ckm', turned_re, inner_sin, precision=HIGHEST)  15.3 us
    dot_general x5, matrix products, spectrum(): jnp.einsum('ckn,nm->ckm', turned_re, inner_cos, precision=HIGHEST)  14.7 us
    all_to_all x1, starting transfers between devices, body(): lax.all_to_all(filter_taps.T.astype(jnp.bfloat16), 'seq', split_axis=0, c...  10.9 us
    all_to_all x1, starting transfers between devices, body(): lax.all_to_all(conv_chan, 'seq', split_axis=1, concat_axis=0, tiled=True)  10.5 us
    all_to_all x1, waiting for transfers between devices, body(): lax.all_to_all(filter_taps.T.astype(jnp.bfloat16), 'seq', split_axis=0, c...  10.4 us
    all_to_all x1, starting transfers between devices, body(): lax.all_to_all(as_sent(grad_kernel), 'seq', split_axis=1, concat_axis=0,...  10.3 us
  transfers between devices with their start and end apart: 12, of which 6 were waited for; matrix products, arithmetic and copies ran while one was open for 37% of the time, Pallas kernels for 0%

commit v1 on v0

v1 whole, which is shorter than its diff:
```python
import functools
import math

import jax
import jax.numpy as jnp
import numpy as np
from jax import lax
from jax.experimental import pallas as pl
from jax.experimental.pallas import tpu as pltpu
from jax.sharding import PartitionSpec as P

MESH = pl.DeviceIdType.MESH
BF16, F32 = jnp.bfloat16, jnp.float32
LANES = 128


def tables(shards, rows):
    outer, full = 2 * shards, 2 * shards * rows
    half = outer // 2 + 1
    padded = -(-half // 8) * 8
    freq, shard, row = np.arange(half), np.arange(shards), np.arange(rows)
    outer_angle = 2 * np.pi * (freq[:, None] * shard[None] % outer) / outer
    twist_angle = 2 * np.pi * (freq[:, None] * row[None] % full) / full
    inner_angle = 2 * np.pi * (row[:, None] * row[None] % rows) / rows
    first = np.zeros((2 * padded, shards))
    first[:half], first[padded : padded + half] = np.cos(outer_angle), -np.sin(outer_angle)
    twist = np.zeros((2, padded, rows))
    twist[0, :half], twist[1, :half] = np.cos(twist_angle), -np.sin(twist_angle)
    cos, sin = np.cos(inner_angle), -np.sin(inner_angle)
    inner = np.block([[cos, sin], [-sin, cos]])
    weight = np.full((half, 1), 2.0 / full)
    weight[0] = weight[-1] = 1.0 / full
    last = np.zeros((shards, 2 * padded))
    last[:, :half] = (weight * np.cos(outer_angle)).T
    last[:, padded : padded + half] = -(weight * np.sin(outer_angle)).T
    as_bf16 = lambda a: jnp.asarray(a.astype(np.float32)).astype(BF16)
    return (
        as_bf16(first),
        jnp.asarray(twist.astype(np.float32)),
        as_bf16(inner),
        as_bf16(inner.T),
        as_bf16(last),
    )


def dot(a, b):
    return jnp.dot(a, b, preferred_element_type=F32)


def enter(n):
    me = lax.axis_index("seq")
    barrier = pltpu.get_barrier_semaphore()

    def greet(i, carry):
        pl.semaphore_signal(
            barrier, inc=1, device_id={"seq": lax.rem(me + i, n)}, device_id_type=MESH
        )
        return carry

    lax.fori_loop(1, n, greet, 0)
    pl.semaphore_wait(barrier, n - 1)
    return me


def exchange_start(me, n, send, recv, sems):
    def push(i, carry):
        peer = lax.rem(me + i, n)
        pltpu.make_async_remote_copy(
            src_ref=send.at[peer],
            dst_ref=recv.at[me],
            send_sem=sems.at[0],
            recv_sem=sems.at[1],
            device_id={"seq": peer},
            device_id_type=MESH,
        ).start()
        return carry

    lax.fori_loop(1, n, push, 0)
    recv[pl.ds(me, 1)] = send[pl.ds(me, 1)]


def whole(me, n, send, recv, sems):
    return pltpu.make_async_remote_copy(
        src_ref=send.at[pl.ds(0, n - 1)],
        dst_ref=recv.at[pl.ds(0, n - 1)],
        send_sem=sems.at[0],
        recv_sem=sems.at[1],
        device_id={"seq": lax.rem(me + 1, n)},
        device_id_type=MESH,
    )


def pack(value, send, n):
    halves = [
        value[h * LANES : (h + 1) * LANES].T.reshape(n, 8, LANES) for h in range(2)
    ]
    send[...] = jnp.concatenate(halves, axis=1).astype(BF16)


def unpack(recv, n):
    value = recv[...].astype(F32)
    return jnp.concatenate(
        [value[:, 8 * h : 8 * h + 8].reshape(8 * n, LANES).T for h in range(2)], axis=0
    )


def spectrum(n, recv, tabs, rowed, mid, out):
    first, twist, inner = tabs[:3]
    padded = twist.shape[1]
    width = twist.shape[2]
    rowed[...] = recv[...].astype(F32).reshape(16 * n, LANES)
    for c in range(8):
        x = jnp.concatenate(
            [rowed[pl.ds(8 * h + c, n, stride=16), :] for h in range(2)], axis=1
        ).astype(BF16)
        a = dot(first[...], x)
        re, im = a[:padded], a[padded:]
        rows = pl.ds(c * padded, padded)
        mid[rows, :width] = re * twist[0] - im * twist[1]
        mid[rows, width:] = re * twist[1] + im * twist[0]
    out[...] = dot(mid[...].astype(BF16), inner[...])


def synthesis(n, tabs, rowed, mid, send):
    twist, back, last = tabs[1], tabs[3], tabs[4]
    padded = twist.shape[1]
    width = twist.shape[2]
    mid[...] = dot(mid[...].astype(BF16), back[...])
    for c in range(8):
        rows = pl.ds(c * padded, padded)
        re, im = mid[rows, :width], mid[rows, width:]
        turned = jnp.concatenate(
            [re * twist[0] + im * twist[1], im * twist[0] - re * twist[1]], axis=0
        ).astype(BF16)
        y = dot(last[...], turned)
        for h in range(2):
            rowed[pl.ds(8 * h + c, n, stride=16), :] = y[:, h * LANES : (h + 1) * LANES]
    send[...] = rowed[...].reshape(n, 16, LANES).astype(BF16)


def front(
    n, query, key, value, taps, short, gain, first, twist, inner, back, last,
    q_out, k_out, v_out, response_out, gate_out, sig_spec, tap_spec,
    ext, halo, rowed, mid, send, recv, halo_sems, sems,
):
    tabs = (first, twist, inner, back, last)
    tokens = query.shape[0]
    me = enter(n)
    streams = (query, key, value)
    edges = []
    for s, stream in enumerate(streams):
        edge = pltpu.make_async_remote_copy(
            src_ref=stream.at[pl.ds(tokens - 16, 16)],
            dst_ref=halo.at[s],
            send_sem=halo_sems.at[0, s],
            recv_sem=halo_sems.at[1, s],
            device_id={"seq": lax.rem(me + 1, n)},
            device_id_type=MESH,
        )
        edge.start()
        edges.append(edge)
    pack(taps[...], send.at[0], n)
    exchange_start(me, n, send.at[0], recv.at[0], sems.at[0])
    shortened = [None] * 3
    for s in (1, 2, 0):
        ext[s, pl.ds(8, tokens)] = streams[s][...].astype(F32)
        edges[s].wait_recv()
        edge_rows = halo[s].astype(F32)[8:]
        ext[s, pl.ds(0, 8)] = jnp.where(me > 0, edge_rows, 0.0)
        shortened[s] = (
            short[s, 0:1, :] * ext[s, pl.ds(8, tokens)]
            + short[s, 1:2, :] * ext[s, pl.ds(7, tokens)]
            + short[s, 2:3, :] * ext[s, pl.ds(6, tokens)]
        ).astype(BF16)
        if s == 2:
            k_out[...] = shortened[1]
            v_out[...] = shortened[2]
            signal = shortened[1].astype(F32) * shortened[2].astype(F32)
            pack(signal, send.at[1], n)
            exchange_start(me, n, send.at[1], recv.at[1], sems.at[1])
            response_out[...] = gain[...] * signal
    q_out[...] = shortened[0]
    whole(me, n, send.at[0], recv.at[0], sems.at[0]).wait_recv()
    spectrum(n, recv.at[0], tabs, rowed, mid, tap_spec)
    whole(me, n, send.at[1], recv.at[1], sems.at[1]).wait_recv()
    spectrum(n, recv.at[1], tabs, rowed, mid, sig_spec)
    width = twist.shape[2]
    ar, ai = tap_spec[:, :width], tap_spec[:, width:]
    br, bi = sig_spec[:, :width], sig_spec[:, width:]
    mid[:, :width] = ar * br - ai * bi
    mid[:, width:] = ar * bi + ai * br
    synthesis(n, tabs, rowed, mid, send.at[2])
    exchange_start(me, n, send.at[2], recv.at[2], sems.at[2])
    whole(me, n, send.at[2], recv.at[2], sems.at[2]).wait_recv()
    response = response_out[...] + unpack(recv.at[2], n)
    response_out[...] = response
    gate_out[...] = (q_out[...].astype(F32) * response).astype(BF16)
    for edge in edges:
        edge.wait_send()
    for i in range(3):
        whole(me, n, send.at[i], recv.at[i], sems.at[i]).wait_send()


def project(gate, weight, grad, mixed, grad_gate):
    part = lax.dot_general(
        grad[...], weight[...], (((1,), (1,)), ((), ())), preferred_element_type=F32
    )

    @pl.when(pl.program_id(0) == 0)
    def _():
        grad_gate[...] = part

    @pl.when(pl.program_id(0) > 0)
    def _():
        grad_gate[...] += part

    mixed[...] = dot(gate[...], weight[...]).astype(BF16)


def rear(
    n, q_short, k_short, v_short, response, grad_gate, short, gain, sig_spec, tap_spec,
    first, twist, inner, back, last,
    query_out, key_out, value_out, taps_out,
    ext, spec, rowed, mid, send, recv, halo_sems, sems,
):
    tabs = (first, twist, inner, back, last)
    tokens = q_short.shape[0]
    width = twist.shape[2]
    me = enter(n)
    grad_response = grad_gate[...] * q_short[...].astype(F32)
    pack(grad_response, send.at[0], n)
    exchange_start(me, n, send.at[0], recv.at[0], sems.at[0])
    ext[0, pl.ds(0, tokens)] = grad_gate[...] * response[...]
    whole(me, n, send.at[0], recv.at[0], sems.at[0]).wait_recv()
    spectrum(n, recv.at[0], tabs, rowed, mid, spec)
    for i, other in ((1, tap_spec), (2, sig_spec)):
        ar, ai = other[:, :width], other[:, width:]
        br, bi = spec[:, :width], spec[:, width:]
        mid[:, :width] = ar * br + ai * bi
        mid[:, width:] = ar * bi - ai * br
        synthesis(n, tabs, rowed, mid, send.at[i])
        exchange_start(me, n, send.at[i], recv.at[i], sems.at[i])
    whole(me, n, send.at[1], recv.at[1], sems.at[1]).wait_recv()
    grad_signal = gain[...] * (grad_gate[...] * q_short[...].astype(F32)) + unpack(
        recv.at[1], n
    )
    ext[1, pl.ds(0, tokens)] = grad_signal * v_short[...].astype(F32)
    ext[2, pl.ds(0, tokens)] = grad_signal * k_short[...].astype(F32)
    edges = []
    for s in range(3):
        edge = pltpu.make_async_remote_copy(
            src_ref=ext.at[s, pl.ds(0, 8)],
            dst_ref=ext.at[s, pl.ds(tokens, 8)],
            send_sem=halo_sems.at[0, s],
            recv_sem=halo_sems.at[1, s],
            device_id={"seq": lax.rem(me + n - 1, n)},
            device_id_type=MESH,
        )
        edge.start()
        edges.append(edge)
    whole(me, n, send.at[2], recv.at[2], sems.at[2]).wait_recv()
    taps_out[...] = unpack(recv.at[2], n) * (1.0 / math.sqrt(tokens * n))
    for s, out in enumerate((query_out, key_out, value_out)):
        edges[s].wait_recv()
        beyond = ext[s, pl.ds(tokens, 8)]
        ext[s, pl.ds(tokens, 8)] = jnp.where(me < n - 1, beyond, 0.0)
        out[...] = (
            short[s, 0:1, :] * ext[s, pl.ds(0, tokens)]
            + short[s, 1:2, :] * ext[s, pl.ds(1, tokens)]
            + short[s, 2:3, :] * ext[s, pl.ds(2, tokens)]
        ).astype(BF16)
    for edge in edges:
        edge.wait_send()
    for i in range(3):
        whole(me, n, send.at[i], recv.at[i], sems.at[i]).wait_send()


def vmem(count):
    return [pl.BlockSpec(memory_space=pltpu.VMEM)] * count


def body(query_in, key_in, value_in, short_filter, skip_gain, filter_taps, out_weight, out_grad):
    n = lax.axis_size("seq")
    tokens, channels = query_in.shape
    features = out_weight.shape[1]
    tabs = tables(n, tokens)
    bins = 8 * tabs[1].shape[1]
    gain = skip_gain[None]
    grads = lax.all_gather(out_grad, "tp", axis=0, tiled=True)
    block = lambda kind: jax.ShapeDtypeStruct((tokens, channels), kind)
    spectra = jax.ShapeDtypeStruct((bins, 2 * tokens), F32)
    scratch = [
        pltpu.VMEM((16 * n, LANES), F32),
        pltpu.VMEM((bins, 2 * tokens), F32),
        pltpu.VMEM((3, n, 16, LANES), BF16),
        pltpu.VMEM((3, n, 16, LANES), BF16),
        pltpu.SemaphoreType.DMA((2, 3)),
        pltpu.SemaphoreType.DMA((3, 2)),
    ]
    limit = 40 * 1024 * 1024
    q_short, k_short, v_short, response, gate, sig_spec, tap_spec = pl.pallas_call(
        functools.partial(front, n),
        out_shape=[block(BF16)] * 3 + [block(F32), block(BF16), spectra, spectra],
        in_specs=vmem(11),
        out_specs=vmem(7),
        scratch_shapes=[
            pltpu.VMEM((3, tokens + 8, channels), F32),
            pltpu.VMEM((3, 16, channels), BF16),
        ]
        + scratch,
        compiler_params=pltpu.CompilerParams(
            collective_id=0, has_side_effects=True, vmem_limit_bytes=limit
        ),
        name="front",
    )(query_in, key_in, value_in, filter_taps, short_filter, gain, *tabs)
    step = 512
    mixed_part, grad_gate = pl.pallas_call(
        project,
        grid=(features // step,),
        out_shape=[jax.ShapeDtypeStruct((tokens, features), BF16), block(F32)],
        in_specs=[
            pl.BlockSpec((tokens, channels), lambda i: (0, 0)),
            pl.BlockSpec((channels, step), lambda i: (0, i)),
            pl.BlockSpec((tokens, step), lambda i: (0, i)),
        ],
        out_specs=[
            pl.BlockSpec((tokens, step), lambda i: (0, i)),
            pl.BlockSpec((tokens, channels), lambda i: (0, 0)),
        ],
        compiler_params=pltpu.CompilerParams(vmem_limit_bytes=limit),
        name="project",
    )(gate, out_weight, grads)
    mixed_out = lax.psum_scatter(mixed_part, "tp", scatter_dimension=0, tiled=True)
    grad_query, grad_key, grad_value, filter_grad = pl.pallas_call(
        functools.partial(rear, n),
        out_shape=[block(BF16)] * 3 + [block(F32)],
        in_specs=vmem(14),
        out_specs=vmem(4),
        scratch_shapes=[
            pltpu.VMEM((3, tokens + 8, channels), F32),
            pltpu.VMEM((bins, 2 * tokens), F32),
        ]
        + scratch,
        compiler_params=pltpu.CompilerParams(
            collective_id=1, has_side_effects=True, vmem_limit_bytes=limit
        ),
        name="rear",
    )(q_short, k_short, v_short, response, grad_gate, short_filter, gain, sig_spec, tap_spec, *tabs)
    return (mixed_out, grad_query, grad_key, grad_value, filter_grad)


def solution(mesh):
    in_specs = (
        P("seq", "tp"),
        P("seq", "tp"),
        P("seq", "tp"),
        P(None, None, "tp"),
        P("tp"),
        P("seq", "tp"),
        P("tp", None),
        P(("seq", "tp"), None),
    )
    out_specs = (
        P(("seq", "tp"), None),
        P("seq", "tp"),
        P("seq", "tp"),
        P("seq", "tp"),
        P("seq", "tp"),
    )
    return jax.shard_map(body, mesh=mesh, in_specs=in_specs, out_specs=out_specs, check_vma=False)
```

time: 276 us -> 127 us (0.46); the launches traced: 271 us -> 126 us
  matrix products: 128 us -> 0 us
  starting transfers between devices: 75.6 us -> 0.08 us
  Pallas kernels: 0 us -> 74.9 us
  waiting for transfers between devices: 30.7 us -> 0.7 us
  local copies, waits for them, and re-layouts: 15.3 us -> 36.1 us
  other arithmetic: 6.35 us -> 0 us
    dot_general x50 -> x0, matrix products: 128 us -> none  [the longest x5 18.5 us: spectrum(): jnp.einsum('ckn,nm->ckm', turned_im, inner_cos, precision=HIGHEST)]
    pallas_call x0 -> x3, Pallas kernels: none -> 74.9 us  [the longest x1 36.6 us: body(): pl.pallas_call(functools.partial(front, n), out_shape=[block(BF16)] * 3 +...]
    all_to_all x8 -> x0, starting transfers between devices: 67.8 us -> none  [the longest x1 10.9 us: body(): lax.all_to_all(filter_taps.T.astype(jnp.bfloat16), 'seq', split_axis=0, c...]
    unnamed x70 -> x72, local copies, waits for them, and re-layouts: 4.58 us -> 36.1 us
    all_to_all x8 -> x0, waiting for transfers between devices: 30.6 us -> none  [the longest x1 10.4 us: body(): lax.all_to_all(filter_taps.T.astype(jnp.bfloat16), 'seq', split_axis=0, c...]
    ppermute x2 -> x0, starting transfers between devices: 7.3 us -> none  [passed_along(): lax.ppermute(value, axis, [(source, source + steps) for source in range(f...]
    convert_element_type x4 -> x0, local copies, waits for them, and re-layouts: 5.28 us -> none  [the longest x1 1.79 us: body(): grad_resp.T.astype(jnp.bfloat16)]
  transfers between devices with their start and end apart: 12 -> 2, of which waited for: 6 -> 0; matrix products, arithmetic and copies ran while one was open for 37% -> 0% of each run, Pallas kernels for 0% -> 54%
where the time goes in v1:
time: 127 us; the launch traced here: 126 us
  Pallas kernels  74.9 us (59%)
  local copies, waits for them, and re-layouts  36.1 us (28%)
  between operations  14.1 us (11%)
    pallas_call x1, Pallas kernels, body(): pl.pallas_call(functools.partial(front, n), out_shape=[block(BF16)] * 3 +...  36.6 us
    unnamed x72, local copies, waits for them, and re-layouts  36.1 us
    pallas_call x1, Pallas kernels, body(): pl.pallas_call(functools.partial(rear, n), out_shape=[block(BF16)] * 3 +...  31.6 us
    pallas_call x1, Pallas kernels, body(): pl.pallas_call(project, grid=(features // step,), out_shape=[jax.ShapeDty...  6.71 us
  transfers between devices with their start and end apart: 2, of which 0 were waited for; matrix products, arithmetic and copies ran while one was open for 0% of the time, Pallas kernels for 54%

profile of v1, /device:TPU:1, one launch (start us, length us, event | category | flops | bytes accessed | tf_op | source)
XLA Modules:
  0.0 125.9 jit_solution(16898977094737784053)
XLA Ops:
  7.2 0.0 all-gather.2.cloned.1.call-start
  7.2 0.7 all-gather.2.cloned.1.call-update
  7.9 0.0 reduce-scatter.2.cloned.1.call-start
  7.9 0.0 copy-start.2
  8.0 1.0 copy-done.2
  9.0 1.0 copy-done.4
  10.0 0.9 copy-done.6
  10.9 1.0 copy-done.13
  12.0 0.9 copy-done.14
  12.9 0.9 copy-done.15
  13.9 0.9 copy-done.16
  14.8 0.8 copy-done.26
  15.6 0.8 copy-done.28
  16.4 0.7 copy-done.30
  17.1 0.7 copy-done.32
  17.8 36.6 %front.1 = (bf16[256,512]{1,0:T(8,128)(2,1)S(1)}, bf16[256,512]{1,0:T(8,128)(2,1)S(1)}, bf16[256,512]{1,0:T(8,128)(2,1)S(1)}, f32[256,512]{1,0:T(8,128)S(1)}, bf...) custom-call(bf16[256,512]{1,0:T(8,128)(2,1)S(1)} %copy-done.14, ...), custom_call_target="tpu_custom_call" | custom-call | tf_op jit(solution)/shard_map/front/pallas_call | solution.py:301
  54.4 0.0 copy-start.8
  54.4 0.8 copy-done.8
  55.2 0.7 copy-done.17
  55.9 0.7 copy-done.19
  56.6 0.7 copy-done.21
  57.3 2.2 %copy-done = bf16[512,4096]{1,0:T(8,128)(2,1)S(1)} copy-done((bf16[512,4096]{1,0:T(8,128)(2,1)S(1)}, bf16[512,4096]{1,0:T(8,128)(2,1)}, u32[]{:S(2)}) %copy-start) | copy-done | bytes 4194328
  59.5 1.6 %copy-done.1 = bf16[256,4096]{1,0:T(8,128)(2,1)S(1)} copy-done((bf16[256,4096]{1,0:T(8,128)(2,1)S(1)}, bf16[256,4096]{1,0:T(8,128)(2,1)}, u32[]{:S(2)}) %copy-start.1) | copy-done | bytes 2097176
  61.1 6.7 %project.1 = (bf16[256,4096]{1,0:T(8,128)(2,1)}, f32[256,512]{1,0:T(8,128)S(1)}) custom-call(bf16[256,512]{1,0:T(8,128)(2,1)S(1)} %get-tuple-element.18.gate, bf16[512,4096]{1,0:T(8,128)(2,1)S(1)} %copy-done, bf16[256,4096]{1,0:T(8,128)(2,1)S(1)} %copy-done.1), custom_call_target="tpu_custom_call" | custom-call | tf_op jit(solution)/shard_map/project/pallas_call | solution.py:317
  67.8 0.8 copy-done.10
  68.6 0.0 reduce-scatter.2.cloned.1.call-update
  68.6 1.0 copy-done.3
  69.6 0.2 copy-done.5
  69.8 0.0 copy-done.7
  69.8 1.0 copy-done.9
  70.9 1.0 copy-done.11
  71.9 0.9 copy-done.18
  72.9 0.9 copy-done.20
  73.8 0.9 copy-done.22
  74.8 0.8 copy-done.27
  75.5 0.8 copy-done.29
  76.3 0.7 copy-done.31
  77.0 0.7 copy-done.33
  77.7 31.6 %rear.1 = (bf16[256,512]{1,0:T(8,128)(2,1)S(1)}, bf16[256,512]{1,0:T(8,128)(2,1)S(1)}, bf16[256,512]{1,0:T(8,128)(2,1)S(1)}, f32[256,512]{1,0:T(8,128)S(1)}) custom-call(bf16[256,512]{1,0:T(8,128)(2,1)S(1)} %copy-done.18, bf16[256,512]{1,0:T(8,128)(2,1)S(1)} %copy-done.20, bf16[256,512]{1,0:T(8,128)(2,1)S(1)} %copy-done.22, f32[256,512]{1,0:T(8,128)S(1)} %copy-done.9, ...), custom_call_target="tpu_custom_call" | custom-call | tf_op jit(solution)/shard_map/rear/pallas_call | solution.py:334
  109.3 0.0 copy-start.12
  109.3 0.8 copy-done.12
  110.1 0.7 copy-done.23
  110.8 0.7 copy-done.24
  111.5 0.7 copy-done.25
  112.2 1.7 %copy.22 = bf16[256,512]{1,0:T(8,128)(2,1)} copy(bf16[256,512]{1,0:T(8,128)(2,1)} %copy-done.25) | data formatting | bytes 524288
  113.9 1.7 %copy.23 = bf16[256,512]{1,0:T(8,128)(2,1)} copy(bf16[256,512]{1,0:T(8,128)(2,1)} %copy-done.24) | data formatting | bytes 524288
  115.6 1.7 %copy.24 = bf16[256,512]{1,0:T(8,128)(2,1)} copy(bf16[256,512]{1,0:T(8,128)(2,1)} %copy-done.23) | data formatting | bytes 524288
  117.2 1.9 %copy.25 = f32[256,512]{1,0:T(8,128)} copy(f32[256,512]{1,0:T(8,128)} %copy-done.12) | data formatting | bytes 1048576
  (33 shorter events, 0.1 us)
Async XLA Ops:
  7.2 50.1 %all-gather.2.cloned.1.call-start = ((), (), s32[]{:S(2)}) async-start(), calls=%async_computation.1 | async-start | bytes 2621440 | tf_op jit(solution)/shard_map/all_gather | solution.py:289
  7.9 104.3 %reduce-scatter.2.cloned.1.call-start = ((), (), s32[]{:S(2)}) async-start(), calls=%async_computation.2 | async-start | bytes 2621440 | tf_op jit(solution)/shard_map/reduce_scatter | solution.py:333
  7.9 1.0 copy-start.2
  9.0 1.0 copy-start.4
  10.0 0.9 copy-start.6
  10.9 1.0 copy-start.13
  12.0 0.9 copy-start.14
  12.9 0.9 copy-start.15
  13.9 0.9 copy-start.16
  14.8 0.8 copy-start.26
  15.6 0.8 copy-start.28
  16.4 0.7 copy-start.30
  17.1 0.7 copy-start.32
  54.4 0.8 copy-start.8
  55.2 0.7 copy-start.17
  55.9 0.7 copy-start.19
  56.6 0.7 copy-start.21
  57.3 2.2 %copy-start = (bf16[512,4096]{1,0:T(8,128)(2,1)S(1)}, bf16[512,4096]{1,0:T(8,128)(2,1)}, u32[]{:S(2)}) copy-start(bf16[512,4096]{1,0:T(8,128)(2,1)} %weight.1) | copy-start | bytes 12582916
  59.5 1.6 %copy-start.1 = (bf16[256,4096]{1,0:T(8,128)(2,1)S(1)}, bf16[256,4096]{1,0:T(8,128)(2,1)}, u32[]{:S(2)}) copy-start(bf16[256,4096]{1,0:T(8,128)(2,1)} %all-gather.2.cloned.1.call-done.grad) | copy-start | bytes 6291460
  67.8 0.8 copy-start.10
  68.6 1.0 copy-start.3
  68.6 1.2 copy-start.5
  68.6 1.2 copy-start.7
  69.8 1.0 copy-start.9
  70.9 1.0 copy-start.11
  71.9 0.9 copy-start.18
  72.9 0.9 copy-start.20
  73.8 0.9 copy-start.22
  74.8 0.8 copy-start.27
  75.5 0.8 copy-start.29
  76.3 0.7 copy-start.31
  77.0 0.7 copy-start.33
  109.3 0.8 copy-start.12
  110.1 0.7 copy-start.23
  110.8 0.7 copy-start.24
  111.5 0.7 copy-start.25
Sparse Core Ops, SparseCore 0:
  9.8 37.1 all-gather.1
  68.7 29.5 reduce-scatter.1

commit v2 on v1

v2 whole, which is shorter than its diff:
```python
import functools
import math

import jax
import jax.numpy as jnp
import numpy as np
from jax import lax
from jax.experimental import pallas as pl
from jax.experimental.pallas import tpu as pltpu
from jax.sharding import PartitionSpec as P

MESH = pl.DeviceIdType.MESH
BF16, F32 = jnp.bfloat16, jnp.float32
LANES = 128


def tables(shards, rows):
    outer, full = 2 * shards, 2 * shards * rows
    half = outer // 2 + 1
    padded = -(-half // 8) * 8
    freq, shard, row = np.arange(half), np.arange(shards), np.arange(rows)
    outer_angle = 2 * np.pi * (freq[:, None] * shard[None] % outer) / outer
    twist_angle = 2 * np.pi * (freq[:, None] * row[None] % full) / full
    inner_angle = 2 * np.pi * (row[:, None] * row[None] % rows) / rows
    first = np.zeros((2 * padded, shards))
    first[:half], first[padded : padded + half] = np.cos(outer_angle), -np.sin(outer_angle)
    twist = np.zeros((2, padded, rows))
    twist[0, :half], twist[1, :half] = np.cos(twist_angle), -np.sin(twist_angle)
    cos, sin = np.cos(inner_angle), -np.sin(inner_angle)
    inner = np.block([[cos, sin], [-sin, cos]])
    weight = np.full((half, 1), 2.0 / full)
    weight[0] = weight[-1] = 1.0 / full
    last = np.zeros((shards, 2 * padded))
    last[:, :half] = (weight * np.cos(outer_angle)).T
    last[:, padded : padded + half] = -(weight * np.sin(outer_angle)).T
    as_bf16 = lambda a: jnp.asarray(a.astype(np.float32)).astype(BF16)
    return (
        as_bf16(first),
        jnp.asarray(twist.astype(np.float32)),
        as_bf16(inner),
        as_bf16(inner.T),
        as_bf16(last),
    )


def dot(a, b):
    return jnp.dot(a, b, preferred_element_type=F32)


def enter(n, m):
    me, part = lax.axis_index("seq"), lax.axis_index("tp")
    barrier = pltpu.get_barrier_semaphore()
    for axis, here, count in (("tp", part, m), ("seq", me, n)):

        def greet(i, carry):
            peer = lax.rem(here + i, count)
            pl.semaphore_signal(barrier, inc=1, device_id={axis: peer}, device_id_type=MESH)
            return carry

        lax.fori_loop(1, count, greet, 0)
    pl.semaphore_wait(barrier, n + m - 2)
    return me, part


def exchange_start(me, n, send, recv, sems):
    def push(i, carry):
        peer = lax.rem(me + i, n)
        pltpu.make_async_remote_copy(
            src_ref=send.at[peer],
            dst_ref=recv.at[me],
            send_sem=sems.at[0],
            recv_sem=sems.at[1],
            device_id={"seq": peer},
            device_id_type=MESH,
        ).start()
        return carry

    lax.fori_loop(1, n, push, 0)
    recv[pl.ds(me, 1)] = send[pl.ds(me, 1)]


def whole(me, n, send, recv, sems):
    return pltpu.make_async_remote_copy(
        src_ref=send.at[pl.ds(0, n - 1)],
        dst_ref=recv.at[pl.ds(0, n - 1)],
        send_sem=sems.at[0],
        recv_sem=sems.at[1],
        device_id={"seq": lax.rem(me + 1, n)},
        device_id_type=MESH,
    )


def pack(value, send, n):
    halves = [
        value[h * LANES : (h + 1) * LANES].T.reshape(n, 8, LANES) for h in range(2)
    ]
    send[...] = jnp.concatenate(halves, axis=1).astype(BF16)


def unpack(recv, n):
    value = recv[...].astype(F32)
    return jnp.concatenate(
        [value[:, 8 * h : 8 * h + 8].reshape(8 * n, LANES).T for h in range(2)], axis=0
    )


def spectrum(n, recv, tabs, rowed, mid, out):
    first, twist, inner = tabs[:3]
    padded = twist.shape[1]
    width = twist.shape[2]
    rowed[...] = recv[...].astype(F32).reshape(16 * n, LANES)
    for c in range(8):
        x = jnp.concatenate(
            [rowed[pl.ds(8 * h + c, n, stride=16), :] for h in range(2)], axis=1
        ).astype(BF16)
        a = dot(first[...], x)
        re, im = a[:padded], a[padded:]
        rows = pl.ds(c * padded, padded)
        mid[rows, :width] = re * twist[0] - im * twist[1]
        mid[rows, width:] = re * twist[1] + im * twist[0]
    out[...] = dot(mid[...].astype(BF16), inner[...])


def synthesis(n, tabs, rowed, mid, send):
    twist, back, last = tabs[1], tabs[3], tabs[4]
    padded = twist.shape[1]
    width = twist.shape[2]
    mid[...] = dot(mid[...].astype(BF16), back[...])
    for c in range(8):
        rows = pl.ds(c * padded, padded)
        re, im = mid[rows, :width], mid[rows, width:]
        turned = jnp.concatenate(
            [re * twist[0] + im * twist[1], im * twist[0] - re * twist[1]], axis=0
        ).astype(BF16)
        y = dot(last[...], turned)
        for h in range(2):
            rowed[pl.ds(8 * h + c, n, stride=16), :] = y[:, h * LANES : (h + 1) * LANES]
    send[...] = rowed[...].reshape(n, 16, LANES).astype(BF16)


def operator(
    n, m, query, key, value, taps_in, short_in, gain_in, weight_in, grad_in,
    first_in, twist_in, inner_in, back_in, last_in,
    mixed_out, query_out, key_out, value_out, taps_out,
    ext, parts, total, results, lags, streams, taps, short, gain, weight, grads, first, twist, inner, back, last,
    halo, beyond, shifted, k_short, v_short, q_short, response, grad_gate, mixed,
    tap_spec, sig_spec, grad_spec, rowed, mid, send, recv,
    load_sems, gather_sems, scatter_sems, halo_sems, beyond_sems, sems, store_sems,
):
    tabs = (first, twist, inner, back, last)
    tokens = query.shape[0]
    width = twist.shape[2]
    own = tokens // m
    chunks, chunk = mixed.shape[0], mixed.shape[2]
    part = lax.axis_index("tp")
    mine = pl.ds(pl.multiple_of(part * own, own), own)
    loads = {}
    for i, (name, source, target) in enumerate((
        ("taps", taps_in, taps),
        ("key", key, streams.at[1]),
        ("value", value, streams.at[2]),
        ("short", short_in, short),
        ("gain", gain_in, gain),
        ("query", query, streams.at[0]),
        ("first", first_in, first),
        ("twist", twist_in, twist),
        ("inner", inner_in, inner),
        ("back", back_in, back),
        ("last", last_in, last),
        ("grad", grad_in, grads.at[mine]),
        ("weight", weight_in, weight),
    )):
        loads[name] = pltpu.make_async_copy(source, target, load_sems.at[i])
        loads[name].start()
    me, part = enter(n, m)

    gathers = []
    for d in (2, 1, 3):
        gathers.append(
            pltpu.make_async_remote_copy(
                src_ref=grad_in,
                dst_ref=grads.at[mine],
                send_sem=gather_sems.at[0, d - 1],
                recv_sem=gather_sems.at[1, d - 1],
                device_id={"tp": lax.rem(part + d, m)},
                device_id_type=MESH,
            )
        )
        gathers[-1].start()
    edges = []
    for s, stream in enumerate((query, key, value)):
        edges.append(
            pltpu.make_async_remote_copy(
                src_ref=stream.at[pl.ds(tokens - 16, 16)],
                dst_ref=halo.at[s],
                send_sem=halo_sems.at[0, s],
                recv_sem=halo_sems.at[1, s],
                device_id={"seq": lax.rem(me + 1, n)},
                device_id_type=MESH,
            )
        )
        edges[-1].start()
    everything = [whole(me, n, send.at[i], recv.at[i], sems.at[i]) for i in range(6)]

    loads["taps"].wait()
    pack(taps[...], send.at[0], n)
    exchange_start(me, n, send.at[0], recv.at[0], sems.at[0])
    loads["short"].wait()
    loads["gain"].wait()

    def shorten(s, name):
        loads[name].wait()
        shifted[pl.ds(8, tokens)] = streams[s].astype(F32)
        edges[s].wait_recv()
        shifted[pl.ds(0, 8)] = jnp.where(me > 0, halo[s].astype(F32)[8:], 0.0)
        return (
            short[s, 0:1, :] * shifted[pl.ds(8, tokens)]
            + short[s, 1:2, :] * shifted[pl.ds(7, tokens)]
            + short[s, 2:3, :] * shifted[pl.ds(6, tokens)]
        ).astype(BF16)

    k_short[...] = shorten(1, "key")
    v_short[...] = shorten(2, "value")
    signal = k_short[...].astype(F32) * v_short[...].astype(F32)
    pack(signal, send.at[1], n)
    exchange_start(me, n, send.at[1], recv.at[1], sems.at[1])
    response[...] = gain[...] * signal
    q_short[...] = shorten(0, "query")
    for name in ("first", "twist", "inner", "back", "last"):
        loads[name].wait()
    everything[0].wait_recv()
    spectrum(n, recv.at[0], tabs, rowed, mid, tap_spec)
    everything[1].wait_recv()
    spectrum(n, recv.at[1], tabs, rowed, mid, sig_spec)
    ar, ai = tap_spec[:, :width], tap_spec[:, width:]
    br, bi = sig_spec[:, :width], sig_spec[:, width:]
    mid[:, :width] = ar * br - ai * bi
    mid[:, width:] = ar * bi + ai * br
    synthesis(n, tabs, rowed, mid, send.at[2])
    exchange_start(me, n, send.at[2], recv.at[2], sems.at[2])

    loads["grad"].wait()
    loads["weight"].wait()
    for gather in gathers:
        gather.wait_recv()
    grad_gate[...] = lax.dot_general(
        grads[...], weight[...], (((1,), (1,)), ((), ())), preferred_element_type=F32
    )
    pack(grad_gate[...] * q_short[...].astype(F32), send.at[3], n)
    exchange_start(me, n, send.at[3], recv.at[3], sems.at[3])

    everything[2].wait_recv()
    response[...] += unpack(recv.at[2], n)
    gate = (q_short[...].astype(F32) * response[...]).astype(BF16)
    scatters = []
    for j in range(chunks):
        mixed[j] = dot(gate, weight[:, j * chunk : (j + 1) * chunk]).astype(BF16)
        for d in (2, 1, 3):
            peer = lax.rem(part + d, m)
            scatters.append(
                pltpu.make_async_remote_copy(
                    src_ref=mixed.at[j, pl.ds(pl.multiple_of(peer * own, own), own)],
                    dst_ref=parts.at[part, j],
                    send_sem=scatter_sems.at[0, j, d - 1],
                    recv_sem=scatter_sems.at[1, j, d - 1],
                    device_id={"tp": peer},
                    device_id_type=MESH,
                )
            )
            scatters[-1].start()
        parts[part, j] = mixed[j, mine]

    forwards = [
        pltpu.make_async_remote_copy(
            src_ref=ext.at[s, pl.ds(0, 8)],
            dst_ref=beyond.at[s],
            send_sem=beyond_sems.at[0, s],
            recv_sem=beyond_sems.at[1, s],
            device_id={"seq": lax.rem(me + n - 1, n)},
            device_id_type=MESH,
        )
        for s in range(3)
    ]
    stores = [
        pltpu.make_async_copy(source, target, store_sems.at[i])
        for i, (source, target) in enumerate((
            (results.at[0], query_out),
            (results.at[1], key_out),
            (results.at[2], value_out),
            (lags, taps_out),
            (total, mixed_out),
        ))
    ]

    def lengthen(s):
        forwards[s].wait_recv()
        ext[s, pl.ds(tokens, 8)] = jnp.where(me < n - 1, beyond[s], 0.0)
        results[s] = (
            short[s, 0:1, :] * ext[s, pl.ds(0, tokens)]
            + short[s, 1:2, :] * ext[s, pl.ds(1, tokens)]
            + short[s, 2:3, :] * ext[s, pl.ds(2, tokens)]
        ).astype(BF16)
        stores[s].start()

    ext[0, pl.ds(0, tokens)] = grad_gate[...] * response[...]
    forwards[0].start()
    everything[3].wait_recv()
    spectrum(n, recv.at[3], tabs, rowed, mid, grad_spec)
    for i, other in ((4, tap_spec), (5, sig_spec)):
        ar, ai = other[:, :width], other[:, width:]
        br, bi = grad_spec[:, :width], grad_spec[:, width:]
        mid[:, :width] = ar * br + ai * bi
        mid[:, width:] = ar * bi - ai * br
        synthesis(n, tabs, rowed, mid, send.at[i])
        exchange_start(me, n, send.at[i], recv.at[i], sems.at[i])
    lengthen(0)
    grad_signal = gain[...] * (grad_gate[...] * q_short[...].astype(F32))
    everything[4].wait_recv()
    grad_signal += unpack(recv.at[4], n)
    ext[1, pl.ds(0, tokens)] = grad_signal * v_short[...].astype(F32)
    forwards[1].start()
    ext[2, pl.ds(0, tokens)] = grad_signal * k_short[...].astype(F32)
    forwards[2].start()
    everything[5].wait_recv()
    lags[...] = unpack(recv.at[5], n) * (1.0 / math.sqrt(tokens * n))
    stores[3].start()
    lengthen(1)
    lengthen(2)
    for scatter in scatters:
        scatter.wait_recv()
    for j in range(chunks):
        added = parts[0, j].astype(F32)
        for p in range(1, m):
            added += parts[p, j].astype(F32)
        total[:, j * chunk : (j + 1) * chunk] = added.astype(BF16)
    stores[4].start()
    for copy in gathers + edges + scatters + everything + forwards:
        copy.wait_send()
    for store in stores:
        store.wait()


def finish(*refs):
    sources, targets, sems = refs[:5], refs[5:10], refs[10]
    copies = [
        pltpu.make_async_copy(source, target, sems.at[i])
        for i, (source, target) in enumerate(zip(sources, targets))
    ]
    for copy in copies:
        copy.start()
    for copy in copies:
        copy.wait()


def hbm(count):
    return [pl.BlockSpec(memory_space=pltpu.HBM)] * count


def body(query_in, key_in, value_in, short_filter, skip_gain, filter_taps, out_weight, out_grad):
    n, m = lax.axis_size("seq"), lax.axis_size("tp")
    tokens, channels = query_in.shape
    features = out_weight.shape[1]
    tabs = tables(n, tokens)
    bins = 8 * tabs[1].shape[1]
    chunks = 4
    own = tokens // m
    kept = pltpu.VMEM
    outputs = (
        [jax.ShapeDtypeStruct((own, features), BF16)]
        + [jax.ShapeDtypeStruct((tokens, channels), BF16)] * 3
        + [jax.ShapeDtypeStruct((tokens, channels), F32)]
    )
    limit = pltpu.CompilerParams(
        collective_id=0, has_side_effects=True, vmem_limit_bytes=58 * 1024 * 1024
    )
    held = pl.pallas_call(
        functools.partial(operator, n, m),
        out_shape=outputs,
        in_specs=hbm(13),
        out_specs=hbm(5),
        scratch_shapes=[
            kept((3, tokens + 8, channels), F32),
            kept((m, chunks, own, features // chunks), BF16),
            kept((own, features), BF16),
            kept((3, tokens, channels), BF16),
            kept((tokens, channels), F32),
            kept((3, tokens, channels), BF16),
            kept((tokens, channels), F32),
            kept(short_filter.shape, F32),
            kept((1, channels), F32),
            kept(out_weight.shape, BF16),
            kept((tokens, features), BF16),
        ]
        + [kept(t.shape, t.dtype) for t in tabs]
        + [
            kept((3, 16, channels), BF16),
            kept((3, 8, channels), F32),
            kept((tokens + 8, channels), F32),
        ]
        + [kept((tokens, channels), BF16)] * 3
        + [kept((tokens, channels), F32)] * 2
        + [kept((chunks, tokens, features // chunks), BF16)]
        + [kept((bins, 2 * tokens), F32)] * 3
        + [
            kept((16 * n, LANES), F32),
            kept((bins, 2 * tokens), F32),
            kept((6, n, 16, LANES), BF16),
            kept((6, n, 16, LANES), BF16),
            pltpu.SemaphoreType.DMA((13,)),
            pltpu.SemaphoreType.DMA((2, m - 1)),
            pltpu.SemaphoreType.DMA((2, chunks, m - 1)),
            pltpu.SemaphoreType.DMA((2, 3)),
            pltpu.SemaphoreType.DMA((2, 3)),
            pltpu.SemaphoreType.DMA((6, 2)),
            pltpu.SemaphoreType.DMA((5,)),
        ],
        compiler_params=limit,
        name="operator",
    )(
        query_in, key_in, value_in, filter_taps, short_filter, skip_gain[None], out_weight,
        out_grad, *tabs,
    )
    return pl.pallas_call(
        finish,
        out_shape=outputs,
        in_specs=hbm(5),
        out_specs=hbm(5),
        scratch_shapes=[pltpu.SemaphoreType.DMA((5,))],
        compiler_params=pltpu.CompilerParams(vmem_limit_bytes=58 * 1024 * 1024),
        name="finish",
    )(*held)


def solution(mesh):
    in_specs = (
        P("seq", "tp"),
        P("seq", "tp"),
        P("seq", "tp"),
        P(None, None, "tp"),
        P("tp"),
        P("seq", "tp"),
        P("tp", None),
        P(("seq", "tp"), None),
    )
    out_specs = (
        P(("seq", "tp"), None),
        P("seq", "tp"),
        P("seq", "tp"),
        P("seq", "tp"),
        P("seq", "tp"),
    )
    return jax.shard_map(body, mesh=mesh, in_specs=in_specs, out_specs=out_specs, check_vma=False)
```

time: 127 us -> 124 us (0.976)
  Pallas kernels: 74.9 us -> 123 us
  local copies, waits for them, and re-layouts: 36.1 us -> 0 us
  between operations: 14.1 us -> 0.64 us
    pallas_call x3 -> x2, Pallas kernels: 74.9 us -> 123 us  [the longest x1 66.3 us: body(): pl.pallas_call(functools.partial(operator, n, m), out_shape=outputs, in_s...]
    unnamed x72 -> x0, local copies, waits for them, and re-layouts: 36.1 us -> none
  transfers between devices with their start and end apart: 2 -> 0, of which waited for: 0 -> 0; matrix products, arithmetic and copies ran while one was open for 0% -> 0% of each run, Pallas kernels for 54% -> 0%
where the time goes in v2:
time: 124 us
  Pallas kernels  123 us (99%)
    pallas_call x1, Pallas kernels, body(): pl.pallas_call(functools.partial(operator, n, m), out_shape=outputs, in_s...  66.3 us
    pallas_call x1, Pallas kernels, body(): pl.pallas_call(finish, out_shape=outputs, in_specs=hbm(5), out_specs=hbm(...  56.7 us

profile of v2, /device:TPU:1, one launch (start us, length us, event | category | flops | bytes accessed | tf_op | source)
XLA Modules:
  0.0 123.6 jit_solution(2442667916806407353)
XLA Ops:
  0.6 66.3 %operator.1 = (bf16[64,4096]{1,0:T(8,128)(2,1)}, bf16[256,512]{1,0:T(8,128)(2,1)}, bf16[256,512]{1,0:T(8,128)(2,1)}, bf16[256,512]{1,0:T(8,128)(2,1)}, f32[256,512]{1,0:T(8,128)}) custom-call(bf16[256,512]{1,0:T(8,128)(2,1)} %query.1, bf16[256,512]{1,0:T(8,128)(2,1)} %key.1, bf16[256,512]{1,0:T(8,128)(2,1)} %value.1, f32[256,512]{1,0:T(8,128)} %taps_in.1, ...), custom_call_target="tpu_custom_call" | custom-call | tf_op jit(solution)/shard_map/operator/pallas_call | solution.py:376
  66.9 56.7 %finish.1 = (bf16[64,4096]{1,0:T(8,128)(2,1)}, bf16[256,512]{1,0:T(8,128)(2,1)}, bf16[256,512]{1,0:T(8,128)(2,1)}, bf16[256,512]{1,0:T(8,128)(2,1)}, f32[256,512]{1,0:T(8,128)}) custom-call(bf16[64,4096]{1,0:T(8,128)(2,1)} %get-tuple-element.10.refs_0_, bf16[256,512]{1,0:T(8,128)(2,1)} %get-tuple-element.11.refs_1_, ...), custom_call_target="tpu_custom_call" | custom-call | tf_op jit(solution)/shard_map/finish/pallas_call | solution.py:423

commit v3 on v2

--- a/solution.py
+++ b/solution.py
@@ -341,15 +341,22 @@
 
 
 def finish(*refs):
-    sources, targets, sems = refs[:5], refs[5:10], refs[10]
-    copies = [
-        pltpu.make_async_copy(source, target, sems.at[i])
-        for i, (source, target) in enumerate(zip(sources, targets))
+    sources, targets, held, sems = refs[:5], refs[5:10], refs[10:15], refs[15]
+    loads = [
+        pltpu.make_async_copy(source, kept, sems.at[0, i])
+        for i, (source, kept) in enumerate(zip(sources, held))
     ]
-    for copy in copies:
-        copy.start()
-    for copy in copies:
-        copy.wait()
+    stores = [
+        pltpu.make_async_copy(kept, target, sems.at[1, i])
+        for i, (kept, target) in enumerate(zip(held, targets))
+    ]
+    for load in loads:
+        load.start()
+    for load, store in zip(loads, stores):
+        load.wait()
+        store.start()
+    for store in stores:
+        store.wait()
 
 
 def hbm(count):
@@ -425,7 +432,8 @@
         out_shape=outputs,
         in_specs=hbm(5),
         out_specs=hbm(5),
-        scratch_shapes=[pltpu.SemaphoreType.DMA((5,))],
+        scratch_shapes=[kept(o.shape, o.dtype) for o in outputs]
+        + [pltpu.SemaphoreType.DMA((2, 5))],
         compiler_params=pltpu.CompilerParams(vmem_limit_bytes=58 * 1024 * 1024),
         name="finish",
     )(*held)

time: 124 us -> 69.4 us (0.56)
  Pallas kernels: 123 us -> 68.6 us
    pallas_call x1, Pallas kernels: 56.7 us -> 2.35 us  [body(): pl.pallas_call(finish, out_shape=outputs, in_specs=hbm(5), out_specs=hbm(...]
where the time goes in v3:
time: 69.4 us; the launch traced here: 69.3 us
  Pallas kernels  68.6 us (99%)
    pallas_call x1, Pallas kernels, body(): pl.pallas_call(functools.partial(operator, n, m), out_shape=outputs, in_s...  66.3 us
    pallas_call x1, Pallas kernels, body(): pl.pallas_call(finish, out_shape=outputs, in_specs=hbm(5), out_specs=hbm(...  2.35 us

profile of v3, /device:TPU:1, one launch (start us, length us, event | category | flops | bytes accessed | tf_op | source)
XLA Modules:
  0.0 69.3 jit_solution(4833008593355188509)
XLA Ops:
  0.6 66.3 %operator.1 = (bf16[64,4096]{1,0:T(8,128)(2,1)}, bf16[256,512]{1,0:T(8,128)(2,1)}, bf16[256,512]{1,0:T(8,128)(2,1)}, bf16[256,512]{1,0:T(8,128)(2,1)}, f32[256,512]{1,0:T(8,128)}) custom-call(bf16[256,512]{1,0:T(8,128)(2,1)} %query.1, bf16[256,512]{1,0:T(8,128)(2,1)} %key.1, bf16[256,512]{1,0:T(8,128)(2,1)} %value.1, f32[256,512]{1,0:T(8,128)} %taps_in.1, ...), custom_call_target="tpu_custom_call" | custom-call | tf_op jit(solution)/shard_map/operator/pallas_call | solution.py:383
  66.9 2.4 %finish.1 = (bf16[64,4096]{1,0:T(8,128)(2,1)}, bf16[256,512]{1,0:T(8,128)(2,1)}, bf16[256,512]{1,0:T(8,128)(2,1)}, bf16[256,512]{1,0:T(8,128)(2,1)}, f32[256,512]{1,0:T(8,128)}) custom-call(bf16[64,4096]{1,0:T(8,128)(2,1)} %get-tuple-element.10.refs_0_, bf16[256,512]{1,0:T(8,128)(2,1)} %get-tuple-element.11.refs_1_, ...), custom_call_target="tpu_custom_call" | custom-call | tf_op jit(solution)/shard_map/finish/pallas_call | solution.py:430

commit v4 on v3

--- a/solution.py
+++ b/solution.py
@@ -47,7 +47,7 @@
     return jnp.dot(a, b, preferred_element_type=F32)
 
 
-def enter(n, m):
+def announce(n, m):
     me, part = lax.axis_index("seq"), lax.axis_index("tp")
     barrier = pltpu.get_barrier_semaphore()
     for axis, here, count in (("tp", part, m), ("seq", me, n)):
@@ -58,7 +58,6 @@
             return carry
 
         lax.fori_loop(1, count, greet, 0)
-    pl.semaphore_wait(barrier, n + m - 2)
     return me, part
 
 
@@ -142,7 +141,7 @@
     n, m, query, key, value, taps_in, short_in, gain_in, weight_in, grad_in,
     first_in, twist_in, inner_in, back_in, last_in,
     mixed_out, query_out, key_out, value_out, taps_out,
-    ext, parts, total, results, lags, streams, taps, short, gain, weight, grads, first, twist, inner, back, last,
+    ext, parts, relayed, summed, total, results, lags, streams, taps, short, gain, weight, grads, first, twist, inner, back, last,
     halo, beyond, shifted, k_short, v_short, q_short, response, grad_gate, mixed,
     tap_spec, sig_spec, grad_spec, rowed, mid, send, recv,
     load_sems, gather_sems, scatter_sems, halo_sems, beyond_sems, sems, store_sems,
@@ -152,7 +151,8 @@
     width = twist.shape[2]
     own = tokens // m
     chunks, chunk = mixed.shape[0], mixed.shape[2]
-    part = lax.axis_index("tp")
+    me, part = announce(n, m)
+    left, right, far = (lax.rem(part + d, m) for d in (3, 1, 2))
     mine = pl.ds(pl.multiple_of(part * own, own), own)
     loads = {}
     for i, (name, source, target) in enumerate((
@@ -172,21 +172,37 @@
     )):
         loads[name] = pltpu.make_async_copy(source, target, load_sems.at[i])
         loads[name].start()
-    me, part = enter(n, m)
-
-    gathers = []
-    for d in (2, 1, 3):
-        gathers.append(
-            pltpu.make_async_remote_copy(
-                src_ref=grad_in,
-                dst_ref=grads.at[mine],
-                send_sem=gather_sems.at[0, d - 1],
-                recv_sem=gather_sems.at[1, d - 1],
-                device_id={"tp": lax.rem(part + d, m)},
-                device_id_type=MESH,
-            )
+    loads["taps"].wait()
+    pack(taps[...], send.at[0], n)
+    pl.semaphore_wait(pltpu.get_barrier_semaphore(), n + m - 2)
+
+    def slab(owner, h):
+        start = owner * own + h * (own // 2)
+        return grads.at[pl.ds(pl.multiple_of(start, own // 2), own // 2)]
+
+    def gather(k, source, owner, h, peer):
+        return pltpu.make_async_remote_copy(
+            src_ref=source,
+            dst_ref=slab(owner, h),
+            send_sem=gather_sems.at[0, k],
+            recv_sem=gather_sems.at[1, k],
+            device_id={"tp": peer},
+            device_id_type=MESH,
         )
-        gathers[-1].start()
+
+    halves = [grad_in.at[pl.ds(h * (own // 2), own // 2)] for h in range(2)]
+    gathers = [
+        gather(0, halves[1], part, 1, right),
+        gather(1, halves[0], part, 0, left),
+        gather(2, halves[0], part, 0, right),
+        gather(3, halves[1], part, 1, left),
+    ]
+    passed = [
+        gather(4, slab(left, 1), left, 1, right),
+        gather(5, slab(right, 0), right, 0, left),
+    ]
+    for copy in gathers:
+        copy.start()
     edges = []
     for s, stream in enumerate((query, key, value)):
         edges.append(
@@ -202,8 +218,6 @@
         edges[-1].start()
     everything = [whole(me, n, send.at[i], recv.at[i], sems.at[i]) for i in range(6)]
 
-    loads["taps"].wait()
-    pack(taps[...], send.at[0], n)
     exchange_start(me, n, send.at[0], recv.at[0], sems.at[0])
     loads["short"].wait()
     loads["gain"].wait()
@@ -230,6 +244,9 @@
         loads[name].wait()
     everything[0].wait_recv()
     spectrum(n, recv.at[0], tabs, rowed, mid, tap_spec)
+    for arrived, copy in zip(gathers[:2], passed):
+        arrived.wait_recv()
+        copy.start()
     everything[1].wait_recv()
     spectrum(n, recv.at[1], tabs, rowed, mid, sig_spec)
     ar, ai = tap_spec[:, :width], tap_spec[:, width:]
@@ -241,8 +258,8 @@
 
     loads["grad"].wait()
     loads["weight"].wait()
-    for gather in gathers:
-        gather.wait_recv()
+    for copy in gathers[2:] + passed:
+        copy.wait_recv()
     grad_gate[...] = lax.dot_general(
         grads[...], weight[...], (((1,), (1,)), ((), ())), preferred_element_type=F32
     )
@@ -252,23 +269,31 @@
     everything[2].wait_recv()
     response[...] += unpack(recv.at[2], n)
     gate = (q_short[...].astype(F32) * response[...]).astype(BF16)
-    scatters = []
-    for j in range(chunks):
+
+    def block(j, owner):
+        return mixed.at[j, pl.ds(pl.multiple_of(owner * own, own), own)]
+
+    def scatter(k, j, source, target, peer):
+        return pltpu.make_async_remote_copy(
+            src_ref=source,
+            dst_ref=target,
+            send_sem=scatter_sems.at[0, j, k],
+            recv_sem=scatter_sems.at[1, j, k],
+            device_id={"tp": peer},
+            device_id_type=MESH,
+        )
+
+    ways = [(left, right, 1) if j < chunks // 2 else (right, left, 0) for j in range(chunks)]
+    relays, directs, sums = [], [], []
+    for j, (way, other, side) in enumerate(ways):
+        relays.append(scatter(0, j, block(j, far), relayed.at[j], way))
+        directs.append(scatter(1, j, block(j, other), parts.at[1 - side, j], other))
+        sums.append(scatter(2, j, summed.at[j], parts.at[side, j], way))
+    order = [j + h * (chunks // 2) for j in range(chunks // 2) for h in range(2)]
+    for j in order:
         mixed[j] = dot(gate, weight[:, j * chunk : (j + 1) * chunk]).astype(BF16)
-        for d in (2, 1, 3):
-            peer = lax.rem(part + d, m)
-            scatters.append(
-                pltpu.make_async_remote_copy(
-                    src_ref=mixed.at[j, pl.ds(pl.multiple_of(peer * own, own), own)],
-                    dst_ref=parts.at[part, j],
-                    send_sem=scatter_sems.at[0, j, d - 1],
-                    recv_sem=scatter_sems.at[1, j, d - 1],
-                    device_id={"tp": peer},
-                    device_id_type=MESH,
-                )
-            )
-            scatters[-1].start()
-        parts[part, j] = mixed[j, mine]
+        relays[j].start()
+        directs[j].start()
 
     forwards = [
         pltpu.make_async_remote_copy(
@@ -313,6 +338,11 @@
         mid[:, width:] = ar * bi - ai * br
         synthesis(n, tabs, rowed, mid, send.at[i])
         exchange_start(me, n, send.at[i], recv.at[i], sems.at[i])
+    for j in order:
+        relays[j].wait_recv()
+        own_term = block(j, ways[j][0])[...].astype(F32)
+        summed[j] = (own_term + relayed[j].astype(F32)).astype(BF16)
+        sums[j].start()
     lengthen(0)
     grad_signal = gain[...] * (grad_gate[...] * q_short[...].astype(F32))
     everything[4].wait_recv()
@@ -326,15 +356,14 @@
     stores[3].start()
     lengthen(1)
     lengthen(2)
-    for scatter in scatters:
-        scatter.wait_recv()
-    for j in range(chunks):
-        added = parts[0, j].astype(F32)
-        for p in range(1, m):
-            added += parts[p, j].astype(F32)
+    for j in order:
+        directs[j].wait_recv()
+        sums[j].wait_recv()
+        added = parts[0, j].astype(F32) + parts[1, j].astype(F32)
+        added += block(j, part)[...].astype(F32)
         total[:, j * chunk : (j + 1) * chunk] = added.astype(BF16)
     stores[4].start()
-    for copy in gathers + edges + scatters + everything + forwards:
+    for copy in gathers + passed + edges + relays + directs + sums + everything + forwards:
         copy.wait_send()
     for store in stores:
         store.wait()
@@ -387,7 +416,9 @@
         out_specs=hbm(5),
         scratch_shapes=[
             kept((3, tokens + 8, channels), F32),
-            kept((m, chunks, own, features // chunks), BF16),
+            kept((2, chunks, own, features // chunks), BF16),
+            kept((chunks, own, features // chunks), BF16),
+            kept((chunks, own, features // chunks), BF16),
             kept((own, features), BF16),
             kept((3, tokens, channels), BF16),
             kept((tokens, channels), F32),
@@ -414,8 +445,8 @@
             kept((6, n, 16, LANES), BF16),
             kept((6, n, 16, LANES), BF16),
             pltpu.SemaphoreType.DMA((13,)),
-            pltpu.SemaphoreType.DMA((2, m - 1)),
-            pltpu.SemaphoreType.DMA((2, chunks, m - 1)),
+            pltpu.SemaphoreType.DMA((2, 6)),
+            pltpu.SemaphoreType.DMA((2, chunks, 3)),
             pltpu.SemaphoreType.DMA((2, 3)),
             pltpu.SemaphoreType.DMA((2, 3)),
             pltpu.SemaphoreType.DMA((6, 2)),

time: 69.4 us -> 63.6 us (0.916)
  Pallas kernels: 68.6 us -> 62.8 us
    pallas_call x1, Pallas kernels: 66.3 us -> 60.5 us  [body(): pl.pallas_call(functools.partial(operator, n, m), out_shape=outputs, in_s...]
where the time goes in v4:
time: 63.6 us; the launch traced here: 63.5 us
  Pallas kernels  62.8 us (99%)
  between operations  0.64 us (1%)
    pallas_call x1, Pallas kernels, body(): pl.pallas_call(functools.partial(operator, n, m), out_shape=outputs, in_s...  60.5 us
    pallas_call x1, Pallas kernels, body(): pl.pallas_call(finish, out_shape=outputs, in_specs=hbm(5), out_specs=hbm(...  2.35 us

profile of v4, /device:TPU:1, one launch (start us, length us, event | category | flops | bytes accessed | tf_op | source)
XLA Modules:
  0.0 63.5 jit_solution(7554634946205564527)
XLA Ops:
  0.6 60.5 %operator.1 = (bf16[64,4096]{1,0:T(8,128)(2,1)}, bf16[256,512]{1,0:T(8,128)(2,1)}, bf16[256,512]{1,0:T(8,128)(2,1)}, bf16[256,512]{1,0:T(8,128)(2,1)}, f32[256,512]{1,0:T(8,128)}) custom-call(bf16[256,512]{1,0:T(8,128)(2,1)} %query.1, bf16[256,512]{1,0:T(8,128)(2,1)} %key.1, bf16[256,512]{1,0:T(8,128)(2,1)} %value.1, f32[256,512]{1,0:T(8,128)} %taps_in.1, ...), custom_call_target="tpu_custom_call" | custom-call | tf_op jit(solution)/shard_map/operator/pallas_call | solution.py:412
  61.1 2.4 %finish.1 = (bf16[64,4096]{1,0:T(8,128)(2,1)}, bf16[256,512]{1,0:T(8,128)(2,1)}, bf16[256,512]{1,0:T(8,128)(2,1)}, bf16[256,512]{1,0:T(8,128)(2,1)}, f32[256,512]{1,0:T(8,128)}) custom-call(bf16[64,4096]{1,0:T(8,128)(2,1)} %get-tuple-element.10.refs_0_, bf16[256,512]{1,0:T(8,128)(2,1)} %get-tuple-element.11.refs_1_, ...), custom_call_target="tpu_custom_call" | custom-call | tf_op jit(solution)/shard_map/finish/pallas_call | solution.py:461

commit v5 on v4

--- a/solution.py
+++ b/solution.py
@@ -61,21 +61,25 @@
     return me, part
 
 
-def exchange_start(me, n, send, recv, sems):
-    def push(i, carry):
-        peer = lax.rem(me + i, n)
-        pltpu.make_async_remote_copy(
-            src_ref=send.at[peer],
-            dst_ref=recv.at[me],
-            send_sem=sems.at[0],
-            recv_sem=sems.at[1],
-            device_id={"seq": peer},
-            device_id_type=MESH,
-        ).start()
-        return carry
-
-    lax.fori_loop(1, n, push, 0)
-    recv[pl.ds(me, 1)] = send[pl.ds(me, 1)]
+def exchange_start(me, n, send, recv, sems, groups=(0, 1), keep=True):
+    for group in groups:
+        odd = lax.rem(me + group, 2)
+
+        def push(i, carry):
+            peer = lax.rem(me + 2 * i + odd, n)
+            pltpu.make_async_remote_copy(
+                src_ref=send.at[peer],
+                dst_ref=recv.at[me],
+                send_sem=sems.at[0],
+                recv_sem=sems.at[1],
+                device_id={"seq": peer},
+                device_id_type=MESH,
+            ).start()
+            return carry
+
+        lax.fori_loop(1 - odd, n // 2, push, 0)
+    if keep and 0 in groups:
+        recv[pl.ds(me, 1)] = send[pl.ds(me, 1)]
 
 
 def whole(me, n, send, recv, sems):
@@ -140,8 +144,8 @@
 def operator(
     n, m, query, key, value, taps_in, short_in, gain_in, weight_in, grad_in,
     first_in, twist_in, inner_in, back_in, last_in,
-    mixed_out, query_out, key_out, value_out, taps_out,
-    ext, parts, relayed, summed, total, results, lags, streams, taps, short, gain, weight, grads, first, twist, inner, back, last,
+    mixed_out, query_out, key_out, value_out, lags,
+    ext, parts, relayed, summed, total, results, streams, taps, short, gain, weight, grads, first, twist, inner, back, last,
     halo, beyond, shifted, k_short, v_short, q_short, response, grad_gate, mixed,
     tap_spec, sig_spec, grad_spec, rowed, mid, send, recv,
     load_sems, gather_sems, scatter_sems, halo_sems, beyond_sems, sems, store_sems,
@@ -201,7 +205,7 @@
         gather(4, slab(left, 1), left, 1, right),
         gather(5, slab(right, 0), right, 0, left),
     ]
-    for copy in gathers:
+    for copy in gathers[:2]:
         copy.start()
     edges = []
     for s, stream in enumerate((query, key, value)):
@@ -216,9 +220,10 @@
             )
         )
         edges[-1].start()
-    everything = [whole(me, n, send.at[i], recv.at[i], sems.at[i]) for i in range(6)]
-
-    exchange_start(me, n, send.at[0], recv.at[0], sems.at[0])
+    landing = [recv.at[i] for i in range(5)] + [lags]
+    everything = [whole(me, n, send.at[i], landing[i], sems.at[i]) for i in range(6)]
+
+    exchange_start(me, n, send.at[0], recv.at[0], sems.at[0], (0,))
     loads["short"].wait()
     loads["gain"].wait()
 
@@ -237,7 +242,11 @@
     v_short[...] = shorten(2, "value")
     signal = k_short[...].astype(F32) * v_short[...].astype(F32)
     pack(signal, send.at[1], n)
-    exchange_start(me, n, send.at[1], recv.at[1], sems.at[1])
+    exchange_start(me, n, send.at[1], recv.at[1], sems.at[1], (0,))
+    exchange_start(me, n, send.at[0], recv.at[0], sems.at[0], (1,))
+    exchange_start(me, n, send.at[1], recv.at[1], sems.at[1], (1,))
+    for copy in gathers[2:]:
+        copy.start()
     response[...] = gain[...] * signal
     q_short[...] = shorten(0, "query")
     for name in ("first", "twist", "inner", "back", "last"):
@@ -312,7 +321,7 @@
             (results.at[0], query_out),
             (results.at[1], key_out),
             (results.at[2], value_out),
-            (lags, taps_out),
+            (send.at[5, me], lags.at[me]),
             (total, mixed_out),
         ))
     ]
@@ -337,7 +346,8 @@
         mid[:, :width] = ar * br + ai * bi
         mid[:, width:] = ar * bi - ai * br
         synthesis(n, tabs, rowed, mid, send.at[i])
-        exchange_start(me, n, send.at[i], recv.at[i], sems.at[i])
+        exchange_start(me, n, send.at[i], landing[i], sems.at[i], keep=i < 5)
+    stores[3].start()
     for j in order:
         relays[j].wait_recv()
         own_term = block(j, ways[j][0])[...].astype(F32)
@@ -351,9 +361,6 @@
     forwards[1].start()
     ext[2, pl.ds(0, tokens)] = grad_signal * k_short[...].astype(F32)
     forwards[2].start()
-    everything[5].wait_recv()
-    lags[...] = unpack(recv.at[5], n) * (1.0 / math.sqrt(tokens * n))
-    stores[3].start()
     lengthen(1)
     lengthen(2)
     for j in order:
@@ -363,25 +370,29 @@
         added += block(j, part)[...].astype(F32)
         total[:, j * chunk : (j + 1) * chunk] = added.astype(BF16)
     stores[4].start()
+    everything[5].wait_recv()
     for copy in gathers + passed + edges + relays + directs + sums + everything + forwards:
         copy.wait_send()
     for store in stores:
         store.wait()
 
 
-def finish(*refs):
-    sources, targets, held, sems = refs[:5], refs[5:10], refs[10:15], refs[15]
+def finish(n, *refs):
+    sources, targets, held, taps, sems = refs[:5], refs[5:10], refs[10:15], refs[15], refs[16]
     loads = [
         pltpu.make_async_copy(source, kept, sems.at[0, i])
         for i, (source, kept) in enumerate(zip(sources, held))
     ]
     stores = [
         pltpu.make_async_copy(kept, target, sems.at[1, i])
-        for i, (kept, target) in enumerate(zip(held, targets))
-    ]
-    for load in loads:
-        load.start()
-    for load, store in zip(loads, stores):
+        for i, (kept, target) in enumerate(zip(held[:4] + (taps,), targets))
+    ]
+    for i in (4, 0, 1, 2, 3):
+        loads[i].start()
+    loads[4].wait()
+    taps[...] = unpack(held[4], n) * (1.0 / math.sqrt(taps.shape[0] * n))
+    stores[4].start()
+    for load, store in zip(loads[:4], stores):
         load.wait()
         store.start()
     for store in stores:
@@ -406,12 +417,13 @@
         + [jax.ShapeDtypeStruct((tokens, channels), BF16)] * 3
         + [jax.ShapeDtypeStruct((tokens, channels), F32)]
     )
+    raw = outputs[:4] + [jax.ShapeDtypeStruct((n, 16, LANES), BF16)]
     limit = pltpu.CompilerParams(
         collective_id=0, has_side_effects=True, vmem_limit_bytes=58 * 1024 * 1024
     )
     held = pl.pallas_call(
         functools.partial(operator, n, m),
-        out_shape=outputs,
+        out_shape=raw,
         in_specs=hbm(13),
         out_specs=hbm(5),
         scratch_shapes=[
@@ -421,7 +433,6 @@
             kept((chunks, own, features // chunks), BF16),
             kept((own, features), BF16),
             kept((3, tokens, channels), BF16),
-            kept((tokens, channels), F32),
             kept((3, tokens, channels), BF16),
             kept((tokens, channels), F32),
             kept(short_filter.shape, F32),
@@ -443,7 +454,7 @@
             kept((16 * n, LANES), F32),
             kept((bins, 2 * tokens), F32),
             kept((6, n, 16, LANES), BF16),
-            kept((6, n, 16, LANES), BF16),
+            kept((5, n, 16, LANES), BF16),
             pltpu.SemaphoreType.DMA((13,)),
             pltpu.SemaphoreType.DMA((2, 6)),
             pltpu.SemaphoreType.DMA((2, chunks, 3)),
@@ -459,11 +470,11 @@
         out_grad, *tabs,
     )
     return pl.pallas_call(
-        finish,
+        functools.partial(finish, n),
         out_shape=outputs,
         in_specs=hbm(5),
         out_specs=hbm(5),
-        scratch_shapes=[kept(o.shape, o.dtype) for o in outputs]
+        scratch_shapes=[kept(o.shape, o.dtype) for o in raw + outputs[4:]]
         + [pltpu.SemaphoreType.DMA((2, 5))],
         compiler_params=pltpu.CompilerParams(vmem_limit_bytes=58 * 1024 * 1024),
         name="finish",

time: 63.6 us -> 61.5 us (0.967)
  Pallas kernels: 62.8 us -> 60.8 us
    pallas_call x2, Pallas kernels: 62.8 us -> 60.8 us  [the longest x1 58.4 us: body(): pl.pallas_call(functools.partial(operator, n, m), out_shape=raw, in_specs...]
where the time goes in v5:
time: 61.5 us; the launch traced here: 61.4 us
  Pallas kernels  60.8 us (99%)
  between operations  0.64 us (1%)
    pallas_call x1, Pallas kernels, body(): pl.pallas_call(functools.partial(operator, n, m), out_shape=raw, in_specs...  58.4 us
    pallas_call x1, Pallas kernels, body(): pl.pallas_call(functools.partial(finish, n), out_shape=outputs, in_specs=...  2.4 us

profile of v5, /device:TPU:1, one launch (start us, length us, event | category | flops | bytes accessed | tf_op | source)
XLA Modules:
  0.0 61.4 jit_solution(3735675845676783419)
XLA Ops:
  0.6 58.4 %operator.1 = (bf16[64,4096]{1,0:T(8,128)(2,1)}, bf16[256,512]{1,0:T(8,128)(2,1)}, bf16[256,512]{1,0:T(8,128)(2,1)}, bf16[256,512]{1,0:T(8,128)(2,1)}, bf16[64,16,128]{2,1,0:T(8,128)(2,1)}) custom-call(bf16[256,512]{1,0:T(8,128)(2,1)} %query.1, bf16[256,512]{1,0:T(8,128)(2,1)} %key.1, bf16[256,512]{1,0:T(8,128)(2,1)} %value.1, f32[256,512]{1,0:T(8,128)} %taps_in.1, ...), custom_call_target="tpu_custom_call" | custom-call | tf_op jit(solution)/shard_map/operator/pallas_call | solution.py:424
  59.0 2.4 %finish.1 = (bf16[64,4096]{1,0:T(8,128)(2,1)}, bf16[256,512]{1,0:T(8,128)(2,1)}, bf16[256,512]{1,0:T(8,128)(2,1)}, bf16[256,512]{1,0:T(8,128)(2,1)}, f32[256,512]{1,0:T(8,128)}) custom-call(bf16[64,4096]{1,0:T(8,128)(2,1)} %get-tuple-element.10.refs_0_, bf16[256,512]{1,0:T(8,128)(2,1)} %get-tuple-element.11.refs_1_, ...), custom_call_target="tpu_custom_call" | custom-call | tf_op jit(solution)/shard_map/finish/pallas_call | solution.py:472

commit v6 on v5

--- a/solution.py
+++ b/solution.py
@@ -57,7 +57,7 @@
             pl.semaphore_signal(barrier, inc=1, device_id={axis: peer}, device_id_type=MESH)
             return carry
 
-        lax.fori_loop(1, count, greet, 0)
+        lax.fori_loop(1, count, greet, 0, unroll=True)
     return me, part
 
 
@@ -155,7 +155,7 @@
     width = twist.shape[2]
     own = tokens // m
     chunks, chunk = mixed.shape[0], mixed.shape[2]
-    me, part = announce(n, m)
+    me, part = lax.axis_index("seq"), lax.axis_index("tp")
     left, right, far = (lax.rem(part + d, m) for d in (3, 1, 2))
     mine = pl.ds(pl.multiple_of(part * own, own), own)
     loads = {}
@@ -176,6 +176,8 @@
     )):
         loads[name] = pltpu.make_async_copy(source, target, load_sems.at[i])
         loads[name].start()
+        if name == "value":
+            announce(n, m)
     loads["taps"].wait()
     pack(taps[...], send.at[0], n)
     pl.semaphore_wait(pltpu.get_barrier_semaphore(), n + m - 2)
@@ -263,7 +265,7 @@
     mid[:, :width] = ar * br - ai * bi
     mid[:, width:] = ar * bi + ai * br
     synthesis(n, tabs, rowed, mid, send.at[2])
-    exchange_start(me, n, send.at[2], recv.at[2], sems.at[2])
+    exchange_start(me, n, send.at[2], recv.at[2], sems.at[2], (1, 0))
 
     loads["grad"].wait()
     loads["weight"].wait()

time: 61.5 us -> 61.5 us (level)
  no operation moved by 1% of the time
where the time goes in v6:
time: 61.5 us; the launch traced here: 61.3 us
  Pallas kernels  60.7 us (99%)
  between operations  0.64 us (1%)
    pallas_call x1, Pallas kernels, body(): pl.pallas_call(functools.partial(operator, n, m), out_shape=raw, in_specs...  58.3 us
    pallas_call x1, Pallas kernels, body(): pl.pallas_call(functools.partial(finish, n), out_shape=outputs, in_specs=...  2.4 us

profile of v6, /device:TPU:1, one launch (start us, length us, event | category | flops | bytes accessed | tf_op | source)
XLA Modules:
  0.0 61.3 jit_solution(1303291469993619003)
XLA Ops:
  0.6 58.3 %operator.1 = (bf16[64,4096]{1,0:T(8,128)(2,1)}, bf16[256,512]{1,0:T(8,128)(2,1)}, bf16[256,512]{1,0:T(8,128)(2,1)}, bf16[256,512]{1,0:T(8,128)(2,1)}, bf16[64,16,128]{2,1,0:T(8,128)(2,1)}) custom-call(bf16[256,512]{1,0:T(8,128)(2,1)} %query.1, bf16[256,512]{1,0:T(8,128)(2,1)} %key.1, bf16[256,512]{1,0:T(8,128)(2,1)} %value.1, f32[256,512]{1,0:T(8,128)} %taps_in.1, ...), custom_call_target="tpu_custom_call" | custom-call | tf_op jit(solution)/shard_map/operator/pallas_call | solution.py:426
  58.9 2.4 %finish.1 = (bf16[64,4096]{1,0:T(8,128)(2,1)}, bf16[256,512]{1,0:T(8,128)(2,1)}, bf16[256,512]{1,0:T(8,128)(2,1)}, bf16[256,512]{1,0:T(8,128)(2,1)}, f32[256,512]{1,0:T(8,128)}) custom-call(bf16[64,4096]{1,0:T(8,128)(2,1)} %get-tuple-element.10.refs_0_, bf16[256,512]{1,0:T(8,128)(2,1)} %get-tuple-element.11.refs_1_, ...), custom_call_target="tpu_custom_call" | custom-call | tf_op jit(solution)/shard_map/finish/pallas_call | solution.py:474

commit v7 on v6

--- a/solution.py
+++ b/solution.py
@@ -111,7 +111,7 @@
     first, twist, inner = tabs[:3]
     padded = twist.shape[1]
     width = twist.shape[2]
-    rowed[...] = recv[...].astype(F32).reshape(16 * n, LANES)
+    rowed[pl.ds(0, 16 * n)] = recv[...].astype(F32).reshape(16 * n, LANES)
     for c in range(8):
         x = jnp.concatenate(
             [rowed[pl.ds(8 * h + c, n, stride=16), :] for h in range(2)], axis=1
@@ -138,7 +138,7 @@
         y = dot(last[...], turned)
         for h in range(2):
             rowed[pl.ds(8 * h + c, n, stride=16), :] = y[:, h * LANES : (h + 1) * LANES]
-    send[...] = rowed[...].reshape(n, 16, LANES).astype(BF16)
+    send[...] = rowed[pl.ds(0, 16 * n)].reshape(n, 16, LANES).astype(BF16)
 
 
 def operator(
@@ -453,7 +453,7 @@
         + [kept((chunks, tokens, features // chunks), BF16)]
         + [kept((bins, 2 * tokens), F32)] * 3
         + [
-            kept((16 * n, LANES), F32),
+            kept((16 * n + 16, LANES), F32),
             kept((bins, 2 * tokens), F32),
             kept((6, n, 16, LANES), BF16),
             kept((5, n, 16, LANES), BF16),

time: 61.5 us -> 61.5 us (level)
  no operation moved by 1% of the time
where the time goes in v7:
time: 61.5 us; the launch traced here: 61.4 us
  Pallas kernels  60.7 us (99%)
  between operations  0.64 us (1%)
    pallas_call x1, Pallas kernels, body(): pl.pallas_call(functools.partial(operator, n, m), out_shape=raw, in_specs...  58.3 us
    pallas_call x1, Pallas kernels, body(): pl.pallas_call(functools.partial(finish, n), out_shape=outputs, in_specs=...  2.4 us

profile of v7, /device:TPU:1, one launch (start us, length us, event | category | flops | bytes accessed | tf_op | source)
XLA Modules:
  0.0 61.4 jit_solution(2250538043672615610)
XLA Ops:
  0.6 58.3 %operator.1 = (bf16[64,4096]{1,0:T(8,128)(2,1)}, bf16[256,512]{1,0:T(8,128)(2,1)}, bf16[256,512]{1,0:T(8,128)(2,1)}, bf16[256,512]{1,0:T(8,128)(2,1)}, bf16[64,16,128]{2,1,0:T(8,128)(2,1)}) custom-call(bf16[256,512]{1,0:T(8,128)(2,1)} %query.1, bf16[256,512]{1,0:T(8,128)(2,1)} %key.1, bf16[256,512]{1,0:T(8,128)(2,1)} %value.1, f32[256,512]{1,0:T(8,128)} %taps_in.1, ...), custom_call_target="tpu_custom_call" | custom-call | tf_op jit(solution)/shard_map/operator/pallas_call | solution.py:426
  59.0 2.4 %finish.1 = (bf16[64,4096]{1,0:T(8,128)(2,1)}, bf16[256,512]{1,0:T(8,128)(2,1)}, bf16[256,512]{1,0:T(8,128)(2,1)}, bf16[256,512]{1,0:T(8,128)(2,1)}, f32[256,512]{1,0:T(8,128)}) custom-call(bf16[64,4096]{1,0:T(8,128)(2,1)} %get-tuple-element.10.refs_0_, bf16[256,512]{1,0:T(8,128)(2,1)} %get-tuple-element.11.refs_1_, ...), custom_call_target="tpu_custom_call" | custom-call | tf_op jit(solution)/shard_map/finish/pallas_call | solution.py:474
